TPU v7x, 32 devices: a whole 2x2x4 slice. The times are simulated.
32 devices in a mesh: stream: 4 (over y, core), batch: 8 (over z, x).
Axes of the slice: x: 2, y: 2, z: 4, core: 2. Of those that a mesh axis runs over, the one named last changes fastest.
Arguments:
- hidden_in: bfloat16 [2, 4, 1024, 768], P(None, 'stream', 'batch'), may hold values from -6 to 6
- norm1_gain: bfloat16 [768], P('batch'), may hold values from 0.5 to 1.5
- w_query: bfloat16 [768, 768], P('batch'), may hold values from -0.078125 to 0.078125
- w_key: bfloat16 [768, 768], P('batch'), may hold values from -0.078125 to 0.078125
- w_value: bfloat16 [768, 768], P('batch'), may hold values from -0.21875 to 0.21875
- w_out: bfloat16 [768, 768], P('batch'), may hold values from -1.25 to 1.25
- rel_table: bfloat16 [384], P('batch'), may hold values from -4 to 4
- norm2_gain: bfloat16 [768], P('batch'), may hold values from 0.5 to 1.5
- w_gate: bfloat16 [768, 2048], P('batch'), may hold values from -0.21875 to 0.21875
- w_up: bfloat16 [768, 2048], P('batch'), may hold values from -0.21875 to 0.21875
- w_down: bfloat16 [2048, 768], P('batch'), may hold values from -0.25 to 0.25
- norm3_gain: bfloat16 [768], P('batch'), may hold values from 0.5 to 1.5
- w_proj: bfloat16 [768, 128], P('batch'), may hold values from -0.21875 to 0.21875
- query_lengths: int32 [2, 2, 32], replicated, may hold values from 8 to 32, as said below
- keyword_request_mask: int32 [2, 2, 32], replicated, may hold values from 0 to 1
- targets: int32 [2, 2, 32], replicated, may hold values from 0 to 7
- candidates: int32 [2, 2, 8, 1024, 8], P(None, None, 'batch'), may hold values from 0 to 127
Outputs:
- vectors: bfloat16 [2, 4, 1024, 128], P(None, 'stream', 'batch')
- grad_hidden: float32 [2, 4, 1024, 768], P(None, 'stream', 'batch')
- grad_norm1_gain: float32 [768], P('batch')
- grad_w_query: float32 [768, 768], P('batch')
- grad_w_key: float32 [768, 768], P('batch')
- grad_w_value: float32 [768, 768], P('batch')
- grad_w_out: float32 [768, 768], P('batch')
- grad_rel_table: float32 [384], P('batch')
- grad_norm2_gain: float32 [768], P('batch')
- grad_w_gate: float32 [768, 2048], P('batch')
- grad_w_up: float32 [768, 2048], P('batch')
- grad_w_down: float32 [2048, 768], P('batch')
- grad_norm3_gain: float32 [768], P('batch')
- grad_w_proj: float32 [768, 128], P('batch')
Inputs may be any that keep to these rules, and one draw needn't show every extreme that they name: `query_lengths`: in every micro-batch and pair some query has exactly 32 tokens and some exactly 8. `targets`: documents are numbered by the batch index of the device that holds them. `candidates`: positions may repeat.
All inputs are finite; a program needn't handle non-finite values.
Results may differ from a plain program's by a relative error of at most 0.025.
Values may be sent and summed in bfloat16 or wider, within the bound.
No kernel may reach another device: no remote copies, remote signals or barrier semaphores. Data moves between devices by JAX's collectives and lax.ppermute only.
A program may use at most 192 MiB of HBM per device.

v0:
```python
import functools
import math

import jax
import jax.numpy as jnp
import numpy as np
from jax import lax
from jax.experimental import pallas as pl
from jax.experimental.pallas import tpu as pltpu
from jax.sharding import PartitionSpec as P

H = 12
DH = 64
BUCKETS = 32
MAX_DIST = 128
DLEN = 128
QLEN = 32
GROUPS = DLEN // QLEN
MICRO = 2
ROWS = MICRO * DLEN
D = 768
FF = 2048
HALF = FF // 2
SHARDS = 8
PIECE_A = 208
PIECE_F = 576
FIRST_A, REST_A = (3, 7), (6, 2, 5, 1, 4, 0)
GROUPS_F = ((6, 7, 2, 3), (4, 5, 0, 1))

EPSILON = 1e-06
HIGHEST = lax.Precision.HIGHEST
BF = jnp.bfloat16
F32 = jnp.float32
EVERY = ("stream", "batch")
MIB = 2**20
ROUND_FLOPS = 5 * 10**10


def distance_bucket(distance):
    half_count = BUCKETS // 2
    exact_count = half_count // 2
    if distance < exact_count:
        return distance
    grown = exact_count + int(
        math.floor(
            math.log(distance / exact_count)
            / math.log(MAX_DIST / exact_count)
            * (half_count - exact_count)
            + 1e-09
        )
    )
    return min(grown, half_count - 1)


def bucket_onehot():
    table = np.zeros((2 * DLEN, BUCKETS), np.float32)
    for o in range(2 * DLEN - 1):
        offset = o - (DLEN - 1)
        table[o, distance_bucket(abs(offset)) + (BUCKETS // 2 if offset > 0 else 0)] = 1.0
    return table


def norm_scale(values):
    return lax.rsqrt(jnp.mean(values * values, axis=-1, keepdims=True) + EPSILON)


def norm_backward(values, gain, grad):
    scale = norm_scale(values)
    pulled = gain * grad
    inner = jnp.mean(values * pulled, axis=-1, keepdims=True)
    back = scale * pulled - values * (scale * scale * scale * inner)
    return back, jnp.sum(grad * values * scale, axis=0, keepdims=True)


def dot(left, right):
    return jnp.dot(left, right, preferred_element_type=F32)


def dot_nt(left, right):
    return lax.dot_general(left, right, (((1,), (1,)), ((), ())), preferred_element_type=F32)


def dot_tn(left, right):
    return lax.dot_general(left, right, (((0,), (0,)), ((), ())), preferred_element_type=F32)


def steps(count, body):
    if count <= 16:
        for i in range(count):
            body(i)
    else:

        @pl.loop(0, count)
        def _(i):
            body(i)


VMEM = pl.BlockSpec(memory_space=pltpu.VMEM)
SMEM = pl.BlockSpec(memory_space=pltpu.SMEM)
HBM = pl.BlockSpec(memory_space=pltpu.HBM)


def positions():
    pairs = lax.axis_size("stream") // 2
    stream = lax.axis_index("stream")
    return lax.axis_index("batch"), stream // pairs, stream % pairs, jnp.where(stream < pairs, 1, 0)


def body_kernel(kernel, lazy, counts, *refs):
    parts = []
    for count in counts:
        parts.append(refs[:count])
        refs = refs[count:]
    arrays, far, outs, far_outs, held, made, scratch = parts
    in_sems, out_sems = refs
    for i, (array, place) in enumerate(zip(arrays, held)):
        pltpu.make_async_copy(array, place, in_sems.at[i]).start()
    sent = set()

    def ready():
        for i, (array, place) in enumerate(zip(arrays, held)):
            pltpu.make_async_copy(array, place, in_sems.at[i]).wait()

    def send(*results):
        for i in results:
            sent.add(i)
            pltpu.make_async_copy(made[i], outs[i], out_sems.at[i]).start()

    if not lazy:
        ready()
    kernel((*positions(), ready, send), *held, *far, *made, *far_outs, *scratch)
    send(*(i for i in range(len(outs)) if i not in sent))
    for i, (place, out) in enumerate(zip(made, outs)):
        pltpu.make_async_copy(place, out, out_sems.at[i]).wait()


def near_kernel(kernel, *refs):
    kernel(positions(), *refs)


def call(
    kernel,
    name,
    arrays,
    outs,
    scratch=(),
    far=(),
    far_outs=(),
    sems=0,
    flops=0,
    limit=59,
    near=False,
    lazy=False,
):
    shapes = [jax.ShapeDtypeStruct(s, t) for s, t in (*outs, *far_outs)]
    moved = sum(math.prod(s.shape) * s.dtype.itemsize for s in shapes)
    moved += sum(math.prod(a.shape) * a.dtype.itemsize for a in (*arrays, *far))
    spaces = [pltpu.VMEM(s, t) for s, t in scratch]
    if sems:
        spaces.append(pltpu.SemaphoreType.DMA((sems,)))
    kind = VMEM if near else HBM
    if near:
        body = functools.partial(near_kernel, kernel)
    else:
        counts = (len(arrays), len(far), len(outs), len(far_outs))
        counts += (len(arrays), len(outs), len(spaces))
        body = functools.partial(body_kernel, kernel, lazy, counts)
        spaces = (
            [pltpu.VMEM(a.shape, a.dtype) for a in arrays]
            + [pltpu.VMEM(s, t) for s, t in outs]
            + spaces
            + [pltpu.SemaphoreType.DMA((max(1, len(part)),)) for part in (arrays, outs)]
        )
    return pl.pallas_call(
        body,
        name=name,
        out_shape=shapes,
        in_specs=[kind] * len(arrays) + [HBM] * len(far),
        out_specs=[kind] * len(outs) + [HBM] * len(far_outs),
        scratch_shapes=spaces,
        compiler_params=pltpu.CompilerParams(vmem_limit_bytes=limit * MIB),
        cost_estimate=pl.CostEstimate(flops=flops, bytes_accessed=moved, transcendentals=0),
    )(*arrays, *far)


def tick_kernel(token, out):
    pass


def tick(token):
    return pl.pallas_call(
        tick_kernel,
        name="tick",
        in_specs=[HBM],
        out_specs=HBM,
        out_shape=jax.ShapeDtypeStruct(token.shape, token.dtype),
        input_output_aliases={0: 0},
        cost_estimate=pl.CostEstimate(flops=ROUND_FLOPS, bytes_accessed=0, transcendentals=0),
    )(token)


def add_kernel(plan, near, far, ids, *refs):
    near, far, refs = refs[:near], refs[near : near + far], refs[near + far :]
    outs, refs = refs[: len(plan)], refs[len(plan) :]
    held, sems = (refs[:-1], refs[-1]) if far else ((), None)
    place = 0
    for entries in plan:
        for terms in entries:
            for is_far, array, entry in terms:
                if is_far:
                    copies([(far[array].at[entry], held[place])], sems.at[place])
                    place += 1
    place = 0
    for out, entries in zip(outs, plan):
        for i, terms in enumerate(entries):
            total = None
            for is_far, array, entry in terms:
                if is_far:
                    landed(held[place], sems.at[place])
                    part = held[place][...].astype(F32)
                    place += 1
                else:
                    part = near[array][entry].astype(F32)
                total = part if total is None else total + part
            out[i] = total.astype(BF)


def base_kernel(picks, whole, ids, own, rest, out, left, right, sems):
    for i, m in enumerate(picks):
        part = rest.at[m if whole else i]
        copies([(own.at[m], left.at[i]), (part, right.at[i])], sems.at[i])
    for i in range(len(picks)):
        landed(left.at[i], sems.at[i])
        landed(right.at[i], sems.at[i])
        left[i] = (left[i].astype(F32) + right[i].astype(F32)).astype(BF)
        copies([(left.at[i], out.at[i])], sems.at[i])
    for i in range(len(picks)):
        landed(left.at[i], sems.at[i])


def base_up(own, rest, picks):
    picks = tuple(picks)
    shape = ((len(picks), *rest.shape[1:]), BF)
    (base,) = call(
        functools.partial(base_kernel, picks, rest.shape[0] > len(picks)),
        "base_up",
        [],
        [],
        [shape, shape],
        far=[own, rest],
        far_outs=[shape],
        sems=len(picks),
    )
    return base


def add_up(*outputs, limit=24):
    known = ([], [])
    plan, flat, shapes = [], [], []
    for entries in outputs:
        plan.append([])
        for terms in entries:
            plan[-1].append([])
            for array, entry in terms:
                is_far = int(array.shape[0] > 4)
                arrays = known[is_far]
                found = [i for i, other in enumerate(arrays) if other is array]
                if not found:
                    arrays.append(array)
                    found = [len(arrays) - 1]
                if is_far:
                    flat.append((array.shape[1:], BF))
                plan[-1][-1].append((is_far, found[0], entry))
        shapes.append(((len(entries), *entries[0][0][0].shape[1:]), BF))
    return call(
        functools.partial(add_kernel, plan, len(known[0]), len(known[1])),
        "add_up",
        known[0],
        shapes,
        flat,
        far=known[1],
        sems=len(flat),
        limit=limit,
        near=True,
    )


def pack_kernel(ids, wq, wk, wv, wo, wg, wu, wd, wp, g1, g2, g3, table, slab_a, slab_f):
    y, core = ids[1], ids[2]

    def fill(top, bottom, wide, rank):
        slab_a[0:96, :] = top[...]
        slab_a[96:192, :] = bottom[...]
        for yy in range(2):

            @pl.when(y == yy)
            def _():
                for k in range(4):
                    start = yy * HALF + k * 256
                    slab_f[k * 96 : (k + 1) * 96, :] = wide[:, start : start + 256]
                row = (2 * yy + rank) * 64
                for k in range(3):
                    slab_f[384 + k * 64 : 384 + (k + 1) * 64, :] = wd[
                        row : row + 64, k * 256 : (k + 1) * 256
                    ]

    @pl.when(core == 0)
    def _():
        fill(wq, wv, wg, 0)
        for k in range(6):
            slab_a[192:208, k * DLEN : (k + 1) * DLEN] = wp[k * 16 : (k + 1) * 16, :]

    @pl.when(core == 1)
    def _():
        fill(wk, wo, wu, 1)
        rows = [g1[...].astype(F32), g2[...].astype(F32), g3[...].astype(F32)]
        head = jnp.concatenate(rows + [jnp.zeros((5, 96), F32)], axis=0)
        tail = jnp.concatenate([table[...].astype(F32), jnp.zeros((7, 48), F32)], axis=0)
        tail = jnp.concatenate([tail, jnp.zeros((8, 48), F32)], axis=1)
        both = jnp.concatenate([head, tail], axis=0)
        slab_a[192:208, :] = jnp.concatenate(
            [both, jnp.zeros((16, D - 96), F32)], axis=1
        ).astype(BF)


def copies(pairs, sem):
    for src, dst in pairs:
        pltpu.make_async_copy(src, dst, sem).start()


def landed(buffer, sem):
    pltpu.make_async_copy(buffer, buffer, sem).wait()


def fetch_a(ids, pieces, spots, wqk, wvo, extra, sems):
    b, core = ids[0], ids[2]
    for cflip, m, array, entry in spots:
        src = pieces[array].at[entry]
        c, j = core ^ cflip, b ^ m
        row = pl.multiple_of(j * 96, 96)
        copies([(src.at[pl.ds(0, 96)], wqk.at[c, pl.ds(row, 96)])], sems.at[0])
        copies([(src.at[pl.ds(96, 96)], wvo.at[c, pl.ds(row, 96)])], sems.at[1])
        copies([(src.at[pl.ds(192, 16)], extra.at[c, j])], sems.at[2])


def fetch_wide(ids, pieces, spots, wgu, sems):
    b, y, core = ids[0], ids[1], ids[2]
    for yflip, cflip, m, array, entry in spots:
        src = pieces[array].at[entry]
        c, yy, j = core ^ cflip, y ^ yflip, b ^ m
        row = pl.multiple_of(j * 96, 96)
        for k in range(4):
            tile = wgu.at[c, yy, pl.ds(row, 96), pl.ds(k * 256, 256)]
            copies([(src.at[pl.ds(k * 96, 96)], tile)], sems.at[2 * yy + c])


def fetch_deep(ids, pieces, spots, wd, sem):
    b, y, core = ids[0], ids[1], ids[2]
    for yflip, cflip, m, array, entry in spots:
        src = pieces[array].at[entry]
        low = pl.multiple_of((b ^ m) * 256 + (2 * (y ^ yflip) + (core ^ cflip)) * 64, 64)
        for k in range(3):
            tile = wd.at[pl.ds(low, 64), pl.ds(k * 256, 256)]
            copies([(src.at[pl.ds(384 + k * 64, 64)], tile)], sem)


def head_masks():
    low_lane = lax.broadcasted_iota(jnp.int32, (DLEN, DLEN), 1) < DH
    return low_lane


def both_heads(pair, low_lane):
    zero = jnp.zeros_like(pair)
    return jnp.concatenate(
        [jnp.where(low_lane, pair, zero), jnp.where(low_lane, zero, pair)], axis=0
    )


PAIRS_OF_HEADS = [
    (m, p, slice(m * DLEN, (m + 1) * DLEN), slice(p * DLEN, (p + 1) * DLEN))
    for m in range(MICRO)
    for p in range(H // 2)
]


def attention_forward_kernel(direct, spots, ids, x, mask, onehot, *refs):
    if direct:
        count = 1 + max(spot[2] for spot in spots)
        pieces, refs = refs[:count], refs[count:]
        qkv, attended, weights, first, n1, n2, gains, wproj, wqk_out, wvo_out = refs[:10]
        wqk, wvo, extra, bias, scores, sems = refs[10:]
        fetch_a(ids, pieces, spots, wqk, wvo, extra, sems)
        ids[4]()
        landed(extra, sems.at[2])
        lane = lax.broadcasted_iota(jnp.int32, (8, D), 1)
        all_gains = jnp.zeros((8, D), F32)
        flat = jnp.zeros((8, D), F32)
        for j in range(SHARDS):
            block = extra[1, j].astype(F32)
            all_gains += pltpu.roll(jnp.where(lane < 96, block[0:8], 0.0), j * 96, 1)
            flat += pltpu.roll(jnp.where(lane < 48, block[8:16], 0.0), j * 48, 1)
            for k in range(6):
                wproj[j * 96 + k * 16 : j * 96 + (k + 1) * 16, :] = extra[
                    0, j, :, k * DLEN : (k + 1) * DLEN
                ]
        gains[...] = all_gains
        ids[5](6, 7)
        flat = flat[0:1, : BUCKETS * H]
    else:
        ids[4]()
        gains, flat_in, wqk, wvo = refs[:4]
        qkv, attended, weights, first, n1, n2, bias, scores = refs[4:]
        flat = flat_in[...].astype(F32)
    entry = lax.broadcasted_iota(jnp.int32, (16, BUCKETS * H), 1)
    head = lax.broadcasted_iota(jnp.int32, (16, BUCKETS * H), 0)
    by_head = jnp.where(entry % H == head, jnp.broadcast_to(flat, entry.shape), 0.0)
    offsets = dot(by_head.astype(BF), onehot[...])
    for h in range(H):
        row = jnp.broadcast_to(offsets[h : h + 1, :], (DLEN, 2 * DLEN))
        rolled = pltpu.roll(row, DLEN + 1, 1, stride=1, stride_axis=0)
        bias[h // 2, (h % 2) * DLEN : (h % 2 + 1) * DLEN, :] = rolled[:, :DLEN]
    tokens = x[...].astype(F32)
    normed = (tokens * norm_scale(tokens) * gains[0:1, :]).astype(BF)
    n1[...] = normed
    if direct:
        landed(wqk, sems.at[0])
        copies([(wqk, wqk_out)], sems.at[0])
        landed(wvo, sems.at[1])
        copies([(wvo, wvo_out)], sems.at[1])
    qkv[0] = dot(normed, wqk[0]).astype(BF)
    qkv[1] = dot(normed, wqk[1]).astype(BF)
    qkv[2] = dot(normed, wvo[0]).astype(BF)
    ids[5](0, 4)
    low_lane = head_masks()
    for i, (m, p, rows, lanes) in enumerate(PAIRS_OF_HEADS):
        scores[i] = dot_nt(both_heads(qkv[0, rows, lanes], low_lane), qkv[1, rows, lanes])
    for i, (m, p, rows, lanes) in enumerate(PAIRS_OF_HEADS):
        hidden = jnp.concatenate([mask[m], mask[m]], axis=0)
        biased = scores[i] + bias[p] + hidden
        shifted = jnp.exp(biased - jnp.max(biased, axis=-1, keepdims=True))
        weights[m, p] = (shifted / jnp.sum(shifted, axis=-1, keepdims=True)).astype(BF)
    ids[5](2)
    for i, (m, p, rows, lanes) in enumerate(PAIRS_OF_HEADS):
        mixed = dot(weights[m, p], qkv[2, rows, lanes])
        attended[rows, lanes] = jnp.where(low_lane, mixed[:DLEN], mixed[DLEN:]).astype(BF)
    ids[5](1)
    x1 = tokens + dot(attended[...], wvo[1])
    first[...] = x1
    ids[5](3)
    n2[...] = (x1 * norm_scale(x1) * gains[1:2, :]).astype(BF)
    if direct:
        landed(wqk, sems.at[0])
        landed(wvo, sems.at[1])


def gelu_parts(gate):
    c0, c1 = math.sqrt(2.0 / math.pi), 0.044715
    square = gate * gate
    bent = jnp.tanh(c0 * gate * (1.0 + c1 * square))
    value = 0.5 * gate * (1.0 + bent)
    slope = 0.5 * (1.0 + bent) + 0.5 * gate * (1.0 - bent * bent) * (
        c0 * (1.0 + 3.0 * c1 * square)
    )
    return value, slope


def ffn_forward_kernel(direct, spots, ids, first, n2, gains, wproj, *refs):
    if direct:
        count = 1 + max(spot[3] for spot in spots)
        pieces, refs = refs[:count], refs[count:]
        second, n3, vectors, gelu_out, slope_out, hidden_out = refs[1:7]
        wgu, wd, gelu_kept, slope_kept, hidden, sems = refs[7:]
        fetch_wide(ids, pieces, spots, wgu, sems)
    else:
        wgu, wd, second, n3, vectors, gelu_kept, slope_kept, hidden = refs
    ids[4]()
    normed = n2[...]
    for step in range(2):
        half = (ids[1] ^ step) if direct else step
        if direct:
            landed(wgu.at[0, half], sems.at[2 * half])
            landed(wgu.at[1, half], sems.at[2 * half + 1])
        gate = dot(normed, wgu[0, half])
        up = dot(normed, wgu[1, half])
        value, slope = gelu_parts(gate)
        gelu_kept[half] = value.astype(BF)
        slope_kept[half] = (up * slope).astype(BF)
        hidden[half] = (value * up).astype(BF)
        if direct and step == 0:
            fetch_deep(ids, pieces, spots, wd, sems.at[4])
        if direct:
            copies([(gelu_kept.at[half], gelu_out.at[half])], sems.at[2 * half])
            copies([(slope_kept.at[half], slope_out.at[half])], sems.at[2 * half + 1])
    if direct:
        landed(wd, sems.at[4])
        copies([(hidden, hidden_out)], sems.at[4])
    total = first[...] + dot(hidden[0], wd[:HALF, :]) + dot(hidden[1], wd[HALF:, :])
    second[...] = total
    ids[5](0)
    normed_three = (total * norm_scale(total) * gains[2:3, :]).astype(BF)
    n3[...] = normed_three
    ids[5](1)
    vectors[...] = dot(normed_three, wproj[...]).astype(BF)
    if direct:
        for half in range(2):
            landed(gelu_kept.at[half], sems.at[2 * half])
            landed(slope_kept.at[half], sems.at[2 * half + 1])
        landed(hidden, sems.at[4])


def count_kernel(ids, picks, counts):
    spots = lax.broadcasted_iota(jnp.int32, (DLEN, DLEN), 0)

    def one(j):
        for m in range(MICRO):
            total = jnp.zeros((DLEN, DLEN), F32)
            for t in range(picks.shape[2]):
                total += jnp.where(spots == picks[m, j, t : t + 1, :], 1.0, 0.0)
            counts[m, j] = total

    steps(picks.shape[1], one)


def block_of(others, m):
    return others[m % 2].at[m // 2] if len(others) == 2 else others[0].at[m]


def group_sums(values):
    lane = lax.broadcasted_iota(jnp.int32, values.shape, 1)
    shift = 1
    while shift < QLEN:
        ahead = pltpu.roll(values, DLEN - shift, 1)
        behind = pltpu.roll(values, shift, 1)
        values = values + jnp.where((lane & shift) == 0, ahead, behind)
        shift *= 2
    return values


def similarity_kernel(direct, count, ids, own, counts, share, *refs):
    others, (soft, score, best) = refs[:-3], refs[-3:]
    b, is_query = ids[0], ids[3]
    scale = DLEN**-0.5

    def one(m):
        j = (b ^ m) if direct else m
        for micro in range(MICRO):
            rows = slice(micro * DLEN, (micro + 1) * DLEN)
            mine, theirs = own[rows, :], block_of(others, m)[rows, :]
            doc = jnp.where(is_query == 1, theirs, mine)
            query = jnp.where(is_query == 1, mine, theirs)
            times = counts[micro, j]
            sim = dot_nt(doc, query) * scale
            peak = jnp.max(jnp.where(times > 0, sim, -jnp.inf), axis=0, keepdims=True)
            mass = jnp.where(times > 0, times * jnp.exp(jnp.minimum(sim - peak, 0.0)), 0.0)
            total = jnp.sum(mass, axis=0, keepdims=True)
            soft[micro, j] = mass / total
            best[micro, pl.ds(j, 1), :] = peak + jnp.log(total)

    steps(count, one)
    for micro in range(MICRO):
        score[micro] = group_sums(best[micro] * share[micro])


def vector_grad_kernel(
    direct, count, ids, soft, share, sharp, target, score, scores, *refs
):
    others, (grad, weight, total) = refs[:-3], refs[-3:]
    b, is_query = ids[0], ids[3]
    scale = DLEN**-0.5

    @pl.when(is_query == 1)
    def _():
        for micro in range(MICRO):
            logits = score[micro] * sharp[micro]
            raised = jnp.exp(logits - jnp.max(logits, axis=0, keepdims=True))
            odds = raised / jnp.sum(raised, axis=0, keepdims=True)
            doc = lax.broadcasted_iota(jnp.int32, (count, DLEN), 0)
            hit = jnp.where(target[micro] == doc, 1.0, 0.0)
            weight[micro] = (odds - hit) * sharp[micro] * share[micro] * scale

    @pl.when(is_query == 0)
    def _():
        for micro in range(MICRO):
            sharpness = sharp[micro]
            logits = scores[:, micro] * sharpness[None]
            peak = jnp.max(logits, axis=0)
            norm = jnp.sum(jnp.exp(logits - peak[None]), axis=0)
            odds = jnp.exp(score[micro] * sharpness - peak) / norm
            hit = jnp.where(target[micro] == b, 1.0, 0.0)
            weight[micro] = (odds - hit) * sharpness * share[micro] * scale

    def parts(m, micro):
        j = (b ^ m) if direct else m
        dense = soft[micro, j] * weight[micro, pl.ds(j, 1), :]
        upper = dense.astype(BF)
        lower = (dense - upper.astype(F32)).astype(BF)
        return upper, lower, block_of(others, m)[micro * DLEN : (micro + 1) * DLEN, :]

    for flag, product in ((1, dot_tn), (0, dot)):

        @pl.when(is_query == flag)
        def _():
            for micro in range(MICRO):
                rows = slice(micro * DLEN, (micro + 1) * DLEN)
                if count <= 16:
                    sums = []
                    for m in range(count):
                        upper, lower, theirs = parts(m, micro)
                        sums.append(product(upper, theirs) + product(lower, theirs))
                    grad[rows, :] = sum(sums[1:], sums[0]).astype(BF)
                else:
                    total[rows, :] = jnp.zeros((DLEN, DLEN), F32)

                    @pl.loop(0, count)
                    def _(m):
                        upper, lower, theirs = parts(m, micro)
                        total[rows, :] += product(upper, theirs) + product(lower, theirs)

                    grad[rows, :] = total[rows, :].astype(BF)


def ffn_backward_kernel(direct, spots, ids, dvec, second, n2, n3, gains, wproj, *refs):
    if direct:
        hidden_in, gelu_in, slope_in = refs[:3]
        count = 1 + max(spot[3] for spot in spots)
        pieces, refs = refs[3 : 3 + count], refs[3 + count :]
        dx2_out, grad_proj, grad_gain, dgu, *outs = refs[:10]
        wd, hidden, gelu_kept, slope_kept, grad_down, quarters, sems = refs[10:]
        fetch_deep(ids, pieces, spots, wd, sems.at[0])
        copies([(slope_in, slope_kept)], sems.at[1])
        copies([(gelu_in, gelu_kept)], sems.at[2])
        copies([(hidden_in, hidden)], sems.at[3])
    else:
        wd, hidden, gelu_kept, slope_kept, dx2_out, grad_proj, grad_gain, dgu, dy_out = refs
    b, y, core, _, ready, send = ids
    ready()
    dvectors = dvec[...]
    dn3 = dot_nt(dvectors, wproj[...])
    dx2, dgain3 = norm_backward(second[...], gains[2:3, :], dn3)
    dx2_out[...] = dx2
    grad_gain[...] = dgain3
    grad_proj[...] = dot_tn(n3[...], dvectors)
    send(0, 1, 2)
    dy = dx2.astype(BF)
    if direct:
        landed(wd, sems.at[0])
    dh = dot_nt(dy, wd[...])
    if direct:
        landed(slope_kept, sems.at[1])
        landed(gelu_kept, sems.at[2])
    for half in range(2):
        part = dh[:, half * HALF : (half + 1) * HALF]
        dgu[0, half] = (part * slope_kept[half].astype(F32)).astype(BF)
        dgu[1, half] = (part * gelu_kept[half].astype(F32)).astype(BF)
    send(3)
    if not direct:
        dy_out[...] = dy
        return
    landed(hidden, sems.at[3])
    normed = n2[...]
    wide_rows, deep_rows = pl.ds(0, 384), pl.ds(384, 192)

    def leave(place, rows):
        if place % 2:
            for group, out in zip(GROUPS_F, outs[1 + place : 3 + place]):
                for i, m in enumerate(group):
                    copies([(quarters.at[place, m, rows], out.at[i, rows])], sems.at[place])
        else:
            copies([(quarters.at[place, :, rows], outs[place // 2].at[:, rows])], sems.at[place])

    for place in (3, 2, 1, 0):
        c, yy = core ^ (place // 2), y ^ (place % 2)
        piece = dot_tn(normed, dgu[c, yy]).astype(BF)
        for j in range(SHARDS):
            for k in range(4):
                quarters[place, b ^ j, k * 96 : (k + 1) * 96, :] = piece[
                    j * 96 : (j + 1) * 96, k * 256 : (k + 1) * 256
                ]
        leave(place, wide_rows)
    for j in range(SHARDS):
        start = (j % 4) * 256
        down = dot_tn(hidden[j // 4, :, start : start + 256], dy).astype(BF)
        for part in range(4):
            grad_down[j, part] = down[part * 64 : (part + 1) * 64, :]
    for place in (3, 2, 1, 0):
        c, yy = core ^ (place // 2), y ^ (place % 2)
        for j in range(SHARDS):
            down = grad_down[j, 2 * yy + c]
            for k in range(3):
                quarters[place, b ^ j, 384 + k * 64 : 384 + (k + 1) * 64, :] = down[
                    :, k * 256 : (k + 1) * 256
                ]
        leave(place, deep_rows)
    for place in range(4):
        landed(quarters.at[place], sems.at[place])


def middle_backward_kernel(direct, spots, ids, dx2, first, dgu, gains, *refs):
    if direct:
        count = 1 + max(spot[3] for spot in spots)
        pieces, refs = refs[:count], refs[count:]
        wvo_in, dx1_out, dattended, grad_gain, wgu, wout, sems = refs
        fetch_wide(ids, pieces, spots, wgu, sems)
        copies([(wvo_in.at[1], wout)], sems.at[4])
    else:
        wgu, wvo, dx1_out, dattended, grad_gain = refs
        wout = wvo.at[1]
    ids[4]()
    dn2 = jnp.zeros((ROWS, D), F32)
    for half in range(2):
        for c in range(2):
            if direct:
                landed(wgu.at[c, half], sems.at[half * 2 + c])
            dn2 = dn2 + dot_nt(dgu[c, half], wgu[c, half])
    back, dgain2 = norm_backward(first[...], gains[1:2, :], dn2)
    dx1 = dx2[...] + back
    dx1_out[...] = dx1
    grad_gain[...] = dgain2
    ids[5](0, 2)
    if direct:
        landed(wout, sems.at[4])
    dattended[...] = dot_nt(dx1.astype(BF), wout[...]).astype(BF)


def attention_backward_kernel(
    direct,
    ids,
    grad_first,
    dattended,
    x,
    n1,
    attended,
    weights,
    qkv,
    gains,
    bucket,
    grad_proj,
    grad_gain2,
    grad_gain3,
    *refs,
):
    if direct:
        wqk_in, wvo_in, grad_in, *outs = refs[:7]
        wqk, wvo, own, other, left, right, dqk, extra, *refs = refs[7:]
        copies([(wvo_in.at[0], wvo.at[0])], refs[-1].at[0])
        copies([(wqk_in, wqk)], refs[-1].at[1])
    else:
        wqk, wvo, small, grad_in, dqkv_out, da_out, left, right, dqk, *refs = refs
    diag, bias_grad, dshares, scaled, queries, douts, *rest = refs
    b, core = ids[0], ids[2]
    ids[4]()
    dx1 = grad_first[...]
    da = dx1.astype(BF)
    low_lane = head_masks()
    row_at = lax.broadcasted_iota(jnp.int32, (DLEN, MICRO * DLEN), 0)
    lane_at = lax.broadcasted_iota(jnp.int32, (DLEN, MICRO * DLEN), 1)
    mirror = jnp.where(row_at == DLEN - 1 - lane_at % DLEN, 1.0, 0.0).astype(BF)
    diag[...] = jnp.zeros_like(diag)
    for i, (m, p, rows, lanes) in enumerate(PAIRS_OF_HEADS):
        queries[i] = both_heads(qkv[0, rows, lanes], low_lane)
        douts[i] = both_heads(dattended[rows, lanes], low_lane)
    for i, (m, p, rows, lanes) in enumerate(PAIRS_OF_HEADS):
        dshares[i] = dot_nt(douts[i], qkv[2, rows, lanes])
        right[0, rows, lanes] = dot_tn(weights[m, p], douts[i]).astype(BF)
    for i, (m, p, rows, lanes) in enumerate(PAIRS_OF_HEADS):
        wide = weights[m, p].astype(F32)
        dshare = dshares[i]
        centre = jnp.sum(wide * dshare, axis=-1, keepdims=True)
        scaled[i] = (wide * (dshare - centre)).astype(BF)
    for i, (m, p, rows, lanes) in enumerate(PAIRS_OF_HEADS):
        dq = dot(scaled[i], qkv[1, rows, lanes])
        dqk[0, rows, lanes] = jnp.where(low_lane, dq[:DLEN], dq[DLEN:]).astype(BF)
        dqk[1, rows, lanes] = dot_tn(scaled[i], queries[i]).astype(BF)
    for h in range(H):
        part = slice((h % 2) * DLEN, (h % 2 + 1) * DLEN)
        both = jnp.concatenate([scaled[m * (H // 2) + h // 2, part] for m in range(MICRO)], axis=0)
        turned = dot(mirror, both)
        wider = jnp.concatenate([turned, jnp.zeros_like(turned)], axis=1)
        rolled = pltpu.roll(wider, 0, 1, stride=1, stride_axis=0)
        diag[h : h + 1, :] = jnp.sum(rolled, axis=0, keepdims=True)
    bias_grad[...] = lax.dot_general(
        bucket[...],
        diag[...],
        (((1,), (1,)), ((), ())),
        precision=HIGHEST,
        preferred_element_type=F32,
    )
    if direct:
        sems = rest[0]
        landed(wvo.at[0], sems.at[0])
        landed(wqk, sems.at[1])
    dn1 = dot_nt(dqk[0], wqk[0]) + dot_nt(dqk[1], wqk[1]) + dot_nt(right[0], wvo[0])
    dx, dgain1 = norm_backward(x[...].astype(F32), gains[0:1, :], dn1)
    grad_in[...] = dx1 + dx
    if direct:
        ids[5](0)
    right[1] = da
    left[0] = n1[...]
    left[1] = attended[...]
    all_gains = jnp.concatenate(
        [dgain1, grad_gain2[...], grad_gain3[...], jnp.zeros((5, D), F32)], axis=0
    )
    if not direct:
        small[0:8, :] = all_gains
        small[8:40, :] = jnp.concatenate(
            [bias_grad[...], jnp.zeros((BUCKETS, D - DLEN), F32)], axis=1
        )
        dqkv_out[0] = dqk[0]
        dqkv_out[1] = dqk[1]
        dqkv_out[2] = right[0]
        da_out[...] = da
        return
    per_shard = BUCKETS // SHARDS
    for j in range(SHARDS):
        for k in range(6):
            extra[0, j, :, k * DLEN : (k + 1) * DLEN] = grad_proj[
                j * 96 + k * 16 : j * 96 + (k + 1) * 16, :
            ]
        extra[1, j] = jnp.zeros((16, D), F32)
        extra[1, j, 0:8, :] = pltpu.roll(all_gains, (D - j * 96) % D, 1)
        extra[1, j, 8 : 8 + per_shard, 0:DLEN] = bias_grad[j * per_shard : (j + 1) * per_shard, :]
    for flip, out in ((1, other), (0, own)):
        c = core ^ flip
        top = dot_tn(n1[...], dqk[c]).astype(BF)
        bottom = dot_tn(left[c], right[c]).astype(BF)
        for j in range(SHARDS):
            m = b ^ j
            out[m, 0:96, :] = top[j * 96 : (j + 1) * 96, :]
            out[m, 96:192, :] = bottom[j * 96 : (j + 1) * 96, :]
            out[m, 192:208, :] = extra[c, j].astype(BF)
        for group, target in zip((FIRST_A, REST_A), outs[2 * flip : 2 * flip + 2]):
            copies([(out.at[m], target.at[i]) for i, m in enumerate(group)], sems.at[flip])
    landed(other, sems.at[1])
    landed(own, sems.at[0])


def finish_wide_kernel(ids, near, far, twin, far_twin, token, grad_g, grad_u, grad_d):
    y, core = ids[1], ids[2]
    for yy in range(2):
        for c in range(2):

            @pl.when((y == yy) & (core == c))
            def _():
                for yflip, cflip, part in ((0, 0, near), (1, 0, far), (0, 1, twin), (1, 1, far_twin)):
                    half, rank = yy ^ yflip, c ^ cflip
                    out = grad_u if rank else grad_g
                    for k in range(4):
                        start = half * HALF + k * 256
                        out[:, start : start + 256] = part[0, k * 96 : (k + 1) * 96, :].astype(F32)
                    low = (2 * half + rank) * 64
                    for k in range(3):
                        grad_d[low : low + 64, k * 256 : (k + 1) * 256] = part[
                            0, 384 + k * 64 : 384 + (k + 1) * 64, :
                        ].astype(F32)


def finish_narrow_kernel(
    ids, near, twin, grad_q, grad_k, grad_v, grad_o, grad_p, grad_1, grad_2, grad_3, table
):
    core = ids[2]
    for c in range(2):

        @pl.when(core == c)
        def _():
            low, high = (twin, near) if c else (near, twin)
            grad_q[...] = low[0, 0:96, :].astype(F32)
            grad_k[...] = high[0, 0:96, :].astype(F32)
            grad_v[...] = low[0, 96:192, :].astype(F32)
            grad_o[...] = high[0, 96:192, :].astype(F32)
            for k in range(6):
                grad_p[k * 16 : (k + 1) * 16, :] = low[
                    0, 192:208, k * DLEN : (k + 1) * DLEN
                ].astype(F32)
            rows = high[0, 192:208, :].astype(F32)
            grad_1[...] = rows[0:1, :96]
            grad_2[...] = rows[1:2, :96]
            grad_3[...] = rows[2:3, :96]
            block = jnp.where(lax.broadcasted_iota(jnp.int32, (8, DLEN), 1) < H, rows[8:16, :DLEN], 0.0)
            line = block[0:1]
            for i in range(1, BUCKETS // SHARDS):
                line += pltpu.roll(block, i * H, 1)[i : i + 1]
            table[...] = line[:, : BUCKETS // SHARDS * H]


def local(
    hidden_in,
    norm1_gain,
    w_query,
    w_key,
    w_value,
    w_out,
    rel_table,
    norm2_gain,
    w_gate,
    w_up,
    w_down,
    norm3_gain,
    w_proj,
    query_lengths,
    keyword_request_mask,
    targets,
    candidates,
):
    streams = lax.axis_size("stream")
    shards = lax.axis_size("batch")
    pairs = streams // 2
    direct = shards == SHARDS and pairs == 2
    b = lax.axis_index("batch")
    s = lax.axis_index("stream")
    y, core = s // pairs, s % pairs
    is_query = s < pairs

    def swap(block, yflip, cflip, m):
        route = []
        for source in range(streams):
            target = ((source // pairs) ^ yflip) * pairs + ((source % pairs) ^ cflip)
            for j in range(shards):
                route.append((source * shards + j, target * shards + (j ^ m)))
        return lax.ppermute(block, EVERY, route)

    micro_count = hidden_in.shape[0]
    slot = jnp.arange(DLEN)
    pair_lengths = lax.dynamic_index_in_dim(query_lengths, core, 1, keepdims=False)
    pair_keyword = lax.dynamic_index_in_dim(keyword_request_mask, core, 1, keepdims=False)
    pair_targets = lax.dynamic_index_in_dim(targets, core, 1, keepdims=False)

    def by_slot(values):
        blocks = values.reshape(micro_count, shards, GROUPS)
        own = lax.dynamic_slice_in_dim(blocks, b, 1, 1)
        blocks = jnp.where(is_query, jnp.broadcast_to(own, blocks.shape), blocks)
        return jnp.repeat(blocks, QLEN, axis=2)

    length_slots = by_slot(pair_lengths)
    valid_slots = (slot % QLEN)[None, None, :] < length_slots
    share = jnp.where(valid_slots, 1.0 / length_slots.astype(F32), 0.0)
    sharp = jnp.where(by_slot(pair_keyword) == 1, 20.0, 10.0).astype(F32)
    target_slots = by_slot(pair_targets)
    own_valid = lax.dynamic_slice_in_dim(valid_slots, b, 1, 1)
    same = (slot[:, None] // QLEN) == (slot[None, :] // QLEN)
    mask = jnp.where(is_query & ~(same[None] & own_valid), -1000000000.0, 0.0).astype(F32)

    small = 16 if direct else 48
    picked = lax.dynamic_index_in_dim(candidates, core, 1, keepdims=False)[:, 0]
    picked = picked.reshape(micro_count, shards, DLEN, picked.shape[-1])
    picked = jnp.transpose(picked, (0, 1, 3, 2))
    received = lax.all_to_all(picked, "batch", split_axis=1, concat_axis=1, tiled=True)
    picks = jnp.where(is_query, received, picked)
    (counts,) = call(
        count_kernel,
        "count",
        [picks],
        [((micro_count, shards, DLEN, DLEN), F32)],
        limit=small,
    )

    fence = lax.optimization_barrier
    first_core = core == 0
    spots_a = spots_f = None
    if direct:
        lines = [part.reshape(1, -1) for part in (norm1_gain, norm2_gain, norm3_gain, rel_table)]
        slab_a, slab_f = call(
            pack_kernel,
            "pack",
            [w_query, w_key, w_value, w_out, w_gate, w_up, w_down, w_proj, *lines],
            [((PIECE_A, D), BF), ((PIECE_F, 256), BF)],
        )

        def join(*parts):
            return jnp.concatenate(parts)

        def along_x(part):
            return swap(part, 0, 0, 1)

        def along_y(part):
            return swap(part, 1, 0, 0)

        def along_z(part):
            return swap(part, 0, 0, 2)

        def along_zz(part):
            return swap(part, 0, 0, 4)

        def other_core(part):
            return swap(part, 0, 1, 0)

        f0, a0 = slab_f[None], slab_a[None]
        token = jnp.zeros((8, DLEN), F32)
        f4, f2, y0, f1, a1 = along_zz(f0), along_z(f0), along_y(f0), along_x(f0), along_x(a0)
        token = tick(token)
        f4, f2, y0, f1, a1, a0, token = fence((f4, f2, y0, f1, a1, a0, token))
        f42, f142, token = fence((join(f4, f2), join(f1, f4, f2), token))
        y142, f53, f6, a4, a2 = (
            along_y(f142),
            along_x(f42),
            along_z(f4),
            along_zz(a0),
            along_z(a0),
        )
        token = tick(token)
        f53, f6, counts, mask, share, sharp, target_slots, token = fence(
            (f53, f6, counts, mask, share, sharp, target_slots, token)
        )
        f65, token = fence((join(f6, f53[0:1]), token))
        f7 = along_x(f6)

        a2, token = fence((a2, token))
        a3 = along_x(a2)
        a4, token = fence((a4, token))
        a5, a6 = along_x(a4), along_z(a4)

        y142, f65, token = fence((y142, f65, token))
        y65 = along_y(f65)

        f7, token = fence((f7, token))
        f37, f_all, token = fence((join(f53[1:2], f7), join(f0, f142, f65, f53[1:2], f7), token))
        f_all, token = fence((f_all, token))
        tf_all = other_core(f_all)

        a6, token = fence((a6, token))
        a7 = along_x(a6)
        a0142, token = fence((join(a0, a1, a4, a2), token))
        ta0142 = other_core(a0142)
        y65, f37, token = fence((y65, f37, token))
        y37, ty65 = along_y(f37), other_core(y65)
        token = tick(token)
        a3, a5, tf_all, ta0142, token = fence((a3, a5, tf_all, ta0142, token))
        a536, y_first, token = fence((join(a5, a3, a6), join(y0, y142), token))
        ta536, ty_first = other_core(a536), other_core(y_first)
        a7, token = fence((a7, token))
        ta7 = other_core(a7)
        token = tick(token)
        y37, ta536, ta7, token = fence((y37, ta536, ta7, token))
        ty37 = other_core(y37)

        order_f = (0, 1, 4, 2, 6, 5, 3, 7)
        groups_a = [
            (0, (a0142, (0, 1, 4, 2)), (a536, (5, 3, 6)), (a7, (7,))),
            (1, (ta0142, (0, 1, 4, 2)), (ta536, (5, 3, 6)), (ta7, (7,))),
        ]
        pieces_a, spots_a, pieces_f, spots_f = [], [], [], []
        for cflip, *group in groups_a:
            for part, flips in group:
                spots_a += [(cflip, m, len(pieces_a), i) for i, m in enumerate(flips)]
                pieces_a.append(part)
    else:

        def whole(part):
            return lax.all_gather(part, "batch", axis=0, tiled=True)

        wqk = jnp.stack([whole(w_query), whole(w_key)])
        wvo = jnp.stack([whole(w_value), whole(w_out)])
        gate_up = jnp.stack([whole(w_gate), whole(w_up)])
        wgu = jnp.transpose(gate_up.reshape(2, D, 2, HALF), (0, 2, 1, 3))
        wd = whole(w_down)
        wproj = whole(w_proj)
        gain_rows = [whole(gain) for gain in (norm1_gain, norm2_gain, norm3_gain)]
        gains = jnp.pad(jnp.stack(gain_rows).astype(F32), ((0, 5), (0, 0)))
        table = whole(rel_table).reshape(1, BUCKETS * H)

    onehot = bucket_onehot()
    by_entry = jnp.asarray(np.repeat(onehot.T, H, axis=0), BF)
    x = hidden_in[:, 0].reshape(ROWS, D)
    row_bf, row_f32 = ((ROWS, D), BF), ((ROWS, D), F32)
    qkv_shape, weight_shape = ((3, ROWS, D), BF), ((MICRO, H // 2, ROWS, DLEN), BF)
    pair_weights = ((2, D, D), BF)
    gain_rows = ((8, D), F32)
    proj_shape = ((D, DLEN), BF)
    kept = [qkv_shape, row_bf, weight_shape, row_f32, row_bf, row_bf]
    bias_shape, score_shape = ((H // 2, ROWS, DLEN), F32), ((H, ROWS, DLEN), F32)
    result = call(
        functools.partial(attention_forward_kernel, direct, spots_a),
        "attention_forward",
        [x, mask, by_entry] + ([] if direct else [gains, table, wqk, wvo]),
        kept + ([gain_rows, proj_shape] if direct else []),
        ([pair_weights, pair_weights, ((2, SHARDS, 16, D), BF)] if direct else [])
        + [bias_shape, score_shape],
        far=pieces_a if direct else [],
        far_outs=[pair_weights, pair_weights] if direct else [],
        sems=3 if direct else 0,
        flops=2 * ROWS * D * D * 4,
        lazy=True,
    )
    qkv, attended, weights, first, n1, n2 = result[:6]
    if direct:
        gains, wproj, wqk, wvo = result[6:]
    first, counts, share, sharp, target_slots = fence((first, counts, share, sharp, target_slots))
    if direct:
        ty_first, ty65, ty37, first, token = fence((ty_first, ty65, ty37, first, token))
        near, twin = ((f_all, order_f),), ((tf_all, order_f),)
        far = ((y_first, order_f[:4]), (y65, order_f[4:6]), (y37, order_f[6:]))
        far_twin = ((ty_first, order_f[:4]), (ty65, order_f[4:6]), (ty37, order_f[6:]))
        for yflip, cflip, group in ((0, 0, near), (0, 1, twin), (1, 0, far), (1, 1, far_twin)):
            for part, flips in group:
                spots_f += [(yflip, cflip, m, len(pieces_f), i) for i, m in enumerate(flips)]
                pieces_f.append(part)
    wide_bf = ((2, ROWS, HALF), BF)
    wgu_shape, wd_shape = ((2, 2, D, HALF), BF), ((FF, D), BF)
    lasting = [wide_bf, wide_bf, wide_bf]
    result = call(
        functools.partial(ffn_forward_kernel, direct, spots_f),
        "ffn_forward",
        [first, n2, gains, wproj] + ([] if direct else [wgu, wd]),
        [row_f32, row_bf, ((ROWS, DLEN), BF)] + ([] if direct else lasting),
        [wgu_shape, wd_shape] + lasting if direct else [],
        far=[*pieces_f, token] if direct else [],
        far_outs=lasting if direct else [],
        sems=5 if direct else 0,
        flops=2 * ROWS * D * FF * 3,
        lazy=True,
    )
    second, n3, vectors, gelu_kept, slope_kept, hidden = result

    if direct:
        even = jnp.stack([swap(vectors, 1, 0, m) for m in (0, 2, 4, 6)])
        others = [even, swap(even, 0, 0, 1)]
    else:
        route = [(i, (i + pairs) % streams) for i in range(streams)]
        arrived = lax.ppermute(vectors, "stream", route)
        others = [lax.all_gather(arrived, "batch", axis=0)]
    block_f32 = ((micro_count, shards, DLEN, DLEN), F32)
    line_f32 = ((micro_count, shards, DLEN), F32)
    soft, score = call(
        functools.partial(similarity_kernel, direct, shards),
        "similarity",
        [vectors, counts, share, *others],
        [block_f32, line_f32],
        [line_f32],
        limit=small,
        near=True,
    )
    if direct:
        blocks = jnp.broadcast_to(score[None], (shards,) + score.shape)
        scores = lax.all_to_all(blocks, "batch", split_axis=0, concat_axis=0, tiled=True)
    else:
        scores = lax.all_gather(score, "batch", axis=0)
    (dvec,) = call(
        functools.partial(vector_grad_kernel, direct, shards),
        "vector_grad",
        [soft, share, sharp, target_slots, score, scores, *others],
        [((ROWS, DLEN), BF)],
        [line_f32, ((ROWS, DLEN), F32)],
        limit=small,
        near=True,
    )

    gain_row = ((1, D), F32)
    proj_f32 = ((D, DLEN), F32)
    dgu_shape = ((2, 2, ROWS, HALF), BF)
    quarter = ((SHARDS, PIECE_F, 256), BF)
    saved = [hidden, gelu_kept, slope_kept]
    result = call(
        functools.partial(ffn_backward_kernel, direct, spots_f),
        "ffn_backward",
        [dvec, second, n2, n3, gains, wproj] + ([] if direct else [wd, *saved]),
        [row_f32, proj_f32, gain_row, dgu_shape] + ([] if direct else [row_bf]),
        [wd_shape, wide_bf, wide_bf, wide_bf, ((SHARDS, 4, 64, D), BF), ((4, *quarter[0]), BF)]
        if direct
        else [],
        far=[*saved, *pieces_f] if direct else [],
        far_outs=[quarter] * 2 + [((4, PIECE_F, 256), BF)] * 4 if direct else [],
        sems=4 if direct else 0,
        flops=2 * ROWS * D * FF * 4,
        lazy=True,
    )
    dx2, grad_proj, grad_gain, dgu = result[:4]
    if direct:
        f_own, f_twin, *f_far = result[4:]
    else:
        dy = result[4]

    if direct:
        def own_f(m, *more):
            group = 0 if m in GROUPS_F[0] else 1
            return [(base_f[group], GROUPS_F[group].index(m)), *more]

        def far_sum(i):
            return [[(f_far[i], n), (c_far[i], n)] for n in range(4)]

        c_far = [other_core(part) for part in f_far[2:]]
        c_far[0], f_twin, dgu = fence((c_far[0], f_twin, dgu))
        twin = other_core(f_twin)
        (sent_a,) = add_up(far_sum(0))
        sent_a, dgu = fence((sent_a, dgu))
        y_a = along_y(sent_a)
    middle_in = [dx2, first, dgu, gains]
    dx1, dattended, grad_gain2 = call(
        functools.partial(middle_backward_kernel, direct, spots_f),
        "middle_backward",
        middle_in + ([] if direct else [wgu, wvo]),
        [row_f32, row_bf, gain_row],
        [wgu_shape, ((D, D), BF)] if direct else [],
        far=[*pieces_f, wvo] if direct else [],
        sems=5 if direct else 0,
        flops=ROUND_FLOPS,
        lazy=True,
    )
    if direct:
        *c_far[1:], twin, dattended = fence((*c_far[1:], twin, dattended))
        (sent_b,) = add_up(far_sum(1))
        base_f = [base_up(f_own, twin, GROUPS_F[0])]
        sent_b, base_f[0], dattended = fence((sent_b, base_f[0], dattended))
    two_rows = ((2, ROWS, D), BF)
    slab_out = ((SHARDS, PIECE_A, D), BF)
    blocks_bf = ((H, ROWS, DLEN), BF)
    result = call(
        functools.partial(attention_backward_kernel, direct),
        "attention_backward",
        [dx1, dattended, x, n1, attended, weights, qkv, gains, jnp.asarray(onehot.T)]
        + [grad_proj, grad_gain2, grad_gain]
        + ([] if direct else [wqk, wvo]),
        [row_f32] if direct else [((40, D), F32), row_f32, qkv_shape, row_bf],
        ([pair_weights, pair_weights, slab_out, slab_out] if direct else [])
        + [two_rows, two_rows, two_rows]
        + ([((2, SHARDS, 16, D), F32)] if direct else [])
        + [((DLEN, 2 * DLEN), F32), ((BUCKETS, DLEN), F32)]
        + [score_shape, blocks_bf, blocks_bf, blocks_bf],
        far=[wqk, wvo] if direct else [],
        far_outs=[((count, PIECE_A, D), BF) for count in (2, 6, 2, 6)] if direct else [],
        sems=2 if direct else 0,
        flops=2 * ROWS * D * D * 7,
        lazy=True,
    )

    if direct:
        input_grad, o_first, o_rest, a_first, a_rest = result

        def own_a(m, *more):
            return [(base_a, REST_A.index(m)), *more]

        o_first, o_rest, a_first, a_rest = fence((o_first, o_rest, a_first, a_rest))
        token = jnp.ones((8, DLEN), F32)
        c_first = other_core(a_first)
        c_first, a_rest, token = fence((c_first, a_rest, token))
        (out_a37,) = add_up([[(o_first, i), (c_first, i)] for i in range(2)])
        out_a37, a_rest, token = fence((out_a37, a_rest, token))
        xa37, c_rest = along_x(out_a37), other_core(a_rest)

        y_a, sent_b, token = fence((y_a, sent_b, token))
        y_b = along_y(sent_b)
        (out_73,) = add_up([own_f(7, (y_a, 1)), own_f(3, (y_a, 3))])
        out_73, token = fence((out_73, token))
        x73 = along_x(out_73)
        token = tick(token)
        c_rest, token = fence((c_rest, token))
        base_a = base_up(o_rest, c_rest, range(len(REST_A)))
        base_f.append(base_up(f_own, twin, GROUPS_F[1]))
        x73, base_a, base_f[1], token = fence((x73, base_a, base_f[1], token))
        (out_62,) = add_up([own_f(6, (y_a, 0), (x73, 0)), own_f(2, (y_a, 2), (x73, 1))])
        out_62, token = fence((out_62, token))
        z62 = along_z(out_62)

        xa37, token = fence((xa37, token))
        out_a51, out_a62 = add_up(
            [own_a(5), own_a(1)], [own_a(6, (xa37, 1)), own_a(2, (xa37, 0))]
        )
        out_a62, token = fence((out_a62, token))
        za62 = along_z(out_a62)

        y_b, token = fence((y_b, token))
        out_5, out_1 = add_up([own_f(5, (y_b, 1))], [own_f(1, (y_b, 3))])
        out_5, token = fence((out_5, token))
        x5 = along_x(out_5)

        x5, z62, token = fence((x5, z62, token))
        (out_4,) = add_up([own_f(4, (y_b, 0), (x5, 0), (z62, 0))])
        out_4, out_a51, out_1, token = fence((out_4, out_a51, out_1, token))
        x1, xa51, z4 = along_x(out_1), along_x(out_a51), along_zz(out_4)

        za62, xa51, token = fence((za62, xa51, token))
        (out_a4,) = add_up([own_a(4, (xa51, 0), (za62, 0))])
        out_a4, token = fence((out_a4, token))
        za4 = along_zz(out_a4)

        x1, z4, token = fence((x1, z4, token))
        (mine_f,) = add_up([own_f(0, (y_b, 2), (x1, 0), (z62, 1), (z4, 0))])
        mine_f, token = fence((mine_f, token))
        far, twin_f = along_y(mine_f), other_core(mine_f)

        za4, token = fence((za4, token))
        (part_a,) = add_up([own_a(0, (xa51, 1), (za62, 1), (za4, 0))])
        part_a, token = fence((part_a, token))
        ya = along_y(part_a)

        far, twin_f, token = fence((far, twin_f, token))
        far_twin_f = other_core(far)
        ya, token = fence((ya, token))
        (mine_a,) = add_up([[(part_a, 0), (ya, 0)]])
        mine_a, far_twin_f, token = fence((mine_a, far_twin_f, token))
        twin_a = other_core(mine_a)
        shard_f32, wide_f32 = ((96, D), F32), ((96, FF), F32)
        grad_g, grad_u, grad_d = call(
            finish_wide_kernel,
            "finish_wide",
            [mine_f, far, twin_f, far_twin_f],
            [wide_f32, wide_f32, ((256, D), F32)],
            far=[token],
            limit=24,
            near=True,
        )
        grad_q, grad_k, grad_v, grad_o, grad_p, *small = call(
            finish_narrow_kernel,
            "finish_narrow",
            [mine_a, twin_a],
            [shard_f32] * 4 + [((96, DLEN), F32), ((1, 96), F32), ((1, 96), F32), ((1, 96), F32)]
            + [((1, 48), F32)],
            limit=24,
            near=True,
        )
        grad_n1, grad_n2, grad_n3, grad_table = [row.reshape(-1) for row in small]
    else:
        small, input_grad, dqkv, da = result

        def summed(part):
            part = lax.psum_scatter(part, "batch", scatter_dimension=0, tiled=True)
            return lax.psum(part, "stream")

        grad_q, grad_k, grad_v = [summed(dot_tn(n1, dqkv[i])) for i in range(3)]
        grad_o = summed(dot_tn(attended, da))
        grad_g, grad_u = [
            summed(jnp.concatenate([dot_tn(n2, dgu[i, half]) for half in range(2)], axis=1))
            for i in range(2)
        ]
        grad_d = summed(jnp.concatenate([dot_tn(hidden[half], dy) for half in range(2)]))
        grad_p = summed(grad_proj)
        grad_n1, grad_n2, grad_n3 = [summed(small[i]) for i in range(3)]
        flat = lax.psum(small[8 : 8 + BUCKETS, :H].reshape(-1), EVERY)
        share_rows = flat.shape[0] // shards
        grad_table = lax.dynamic_slice_in_dim(flat, b * share_rows, share_rows, 0)

    vectors_out = vectors.reshape(micro_count, DLEN, DLEN)[:, None]
    grad_hidden = input_grad.reshape(micro_count, DLEN, D)[:, None]
    return (
        vectors_out,
        grad_hidden,
        grad_n1,
        grad_q,
        grad_k,
        grad_v,
        grad_o,
        grad_table,
        grad_n2,
        grad_g,
        grad_u,
        grad_d,
        grad_n3,
        grad_p,
    )


def solution(mesh):
    rows, lines = P("batch", None), P("batch")
    spread = P(None, "stream", "batch", None)
    return jax.shard_map(
        local,
        mesh=mesh,
        in_specs=(spread, lines, rows, rows, rows, rows, lines, lines, rows, rows, rows, lines, rows)
        + (P(), P(), P(), P(None, None, "batch", None, None)),
        out_specs=(spread, spread, lines, rows, rows, rows, rows, lines, lines)
        + (rows, rows, rows, lines, rows),
        check_vma=False,
    )
```

profile of v0, /device:TPU:1, one launch (start us, length us, event | category | flops | bytes accessed | tf_op | source)
XLA Modules:
  0.0 259.8 jit_solution(16090611518412093599)
XLA Ops:
  0.7 2.6 pack.1
  3.3 3.2 %collective-permute-start = (bf16[1,576,256]{2,1,0:T(8,128)(2,1)}, bf16[1,576,256]{2,1,0:T(8,128)(2,1)}, u32[]{:S(2)}, u32[]{:S(2)}) collective-permute-start(bf16[1,576,256]{2,1,0:T(8,128)(2,1)} %bitcast.41), channel_id=1, source_target_pairs={{0,4},{1,5},{2,6},{3,7},{4,0},{5,1},{6,2},{7,3},{8,12},{9,13},{10,... | collective-permute-start | bytes 884744 | tf_op jit(solution)/shard_map/ppermute | solution.py:919
  10.9 3.4 %all-to-all-start = ((s32[2,8,8,128]{3,2,0,1:T(8,128)}), s32[2,8,8,128]{3,2,0,1:T(8,128)S(1)}, u32[]{:S(2)}, u32[]{:S(2)}) async-start(s32[2,8,8,128]{3,2,0,1:T(8,128)} %copy.42), calls=%async_computation | async-start | bytes 131072 | tf_op jit(solution)/shard_map/all_to_all | solution.py:946
  18.9 3.6 %all-to-all-done = s32[2,8,8,128]{3,2,0,1:T(8,128)S(1)} async-done(((s32[2,8,8,128]{3,2,0,1:T(8,128)}), s32[2,8,8,128]{3,2,0,1:T(8,128)S(1)}, u32[]{:S(2)}, u32[]{:S(2)}) %all-to-all-start) | async-done | bytes 65568 | tf_op jit(solution)/shard_map/all_to_all | solution.py:946
  24.8 1.9 collective-permute-start.9
  27.3 1.9 pad_maximum_fusion.4
  29.2 2.2 pad_maximum_fusion.3
  34.5 12.3 %collective-permute-done.7 = bf16[1,576,256]{2,1,0:T(8,128)(2,1)} collective-permute-done((bf16[1,576,256]{2,1,0:T(8,128)(2,1)}, bf16[1,576,256]{2,1,0:T(8,128)(2,1)}, u32[]{:S(2)}, u32[]{:S(2)}) %collective-permute-start.7) | collective-permute-done | bytes 294944 | tf_op jit(solution)/shard_map/ppermute | solution.py:919
  51.4 2.4 pad_maximum_fusion.refs_3_
  57.1 4.3 %collective-permute-start.13 = (bf16[8,576,256]{2,1,0:T(8,128)(2,1)S(1)}, bf16[8,576,256]{2,1,0:T(8,128)(2,1)}, u32[]{:S(2)}, u32[]{:S(2)}) collective-permute-start(bf16[8,576,256]{2,1,0:T(8,128)(2,1)S(1)} %constant_dynamic-update-slice_fusion.refs_4_.refs_9_), channel_id=1, source_target_pairs={{0,8},{1,9},{2,10},{3,11},{4,12},{5,13},{6,14},{7,15},{8,0},{9,1},... | collective-permute-start | bytes 7077896 | tf_op jit(solution)/shard_map/ppermute | solution.py:919
  61.4 2.4 pad_maximum_fusion.1.refs_6_.refs_11_
  63.8 2.1 collective-permute-done.16.refs_7_.refs_12_
  66.7 2.2 collective-permute-done.8
  68.8 4.2 %collective-permute-start.18 = (bf16[2,576,256]{2,1,0:T(8,128)(2,1)}, bf16[2,576,256]{2,1,0:T(8,128)(2,1)}, u32[]{:S(2)}, u32[]{:S(2)}) collective-permute-start(bf16[2,576,256]{2,1,0:T(8,128)(2,1)} %collective-permute-done.16.refs_7_.refs_12_), channel_id=1, source_target_pairs={{0,8},{1,9},{2,10},{3,11},{4,12},{5,13},{6,14},{7,15},{8,0},{9,1},... | collective-permute-start | bytes 1769480 | tf_op jit(solution)/shard_map/ppermute | solution.py:919
  75.3 2.7 %collective-permute-start.22 = (bf16[1,208,768]{2,1,0:T(8,128)(2,1)}, bf16[1,208,768]{2,1,0:T(8,128)(2,1)S(1)}, u32[]{:S(2)}, u32[]{:S(2)}) collective-permute-start(bf16[1,208,768]{2,1,0:T(8,128)(2,1)} %collective-permute-done.21.refs_5_), channel_id=1, source_target_pairs={{0,8},{1,9},{2,10},{3,11},{4,12},{5,13},{6,14},{7,15},{8,0},{9,1},... | collective-permute-start | bytes 958472 | tf_op jit(solution)/shard_map/ppermute | solution.py:919
  80.0 2.1 collective-permute-done.20.refs_7_
  82.8 7.2 %attention_forward.1 = (bf16[3,256,768]{2,1,0:T(8,128)(2,1)}, bf16[256,768]{1,0:T(8,128)(2,1)}, bf16[2,6,256,128]{3,2,1,0:T(8,128)(2,1)}, f32[256,768]{1,0:T(8,1...) custom-call(bf16[256,768]{1,0:T(8,128)(2,1)} %bitcast.35, ...), custom_call_target="tpu_custom_call" | custom-call | flops 1207959552 | bytes 14704640 | tf_op jit(solution)/shard_map/attention_forward/pallas_call | solution.py:174
  91.3 9.2 %ffn_forward.1 = (f32[256,768]{1,0:T(8,128)}, bf16[256,768]{1,0:T(8,128)(2,1)}, bf16[256,128]{1,0:T(8,128)(2,1)}, bf16[2,256,1024]{2,1,0:T(8,128)(2,1)}, bf16[2,...) custom-call(f32[256,768]{1,0:T(8,128)} %get-tuple-element.262.refs_0_.refs_1_, ...), custom_call_target="tpu_custom_call" | custom-call | flops 2415919104 | bytes 15233024 | tf_op jit(solution)/shard_map/ffn_forward/pallas_call | solution.py:174
  100.5 2.6 collective-permute-start.25
  104.5 1.6 collective-permute-start.27
  106.2 2.6 collective-permute-done.26
  108.7 1.8 collective-permute-done.27
  111.7 4.1 %collective-permute-done.28.refs_4_.refs_7_ = bf16[4,256,128]{2,1,0:T(8,128)(2,1)S(1)} collective-permute-done((bf16[4,256,128]{2,1,0:T(8,128)(2,1)S(1)}, bf16[4,256,128]{2,1,0:T(8,128)(2,1)S(1)}, u32[]{:S(2)}, u32[]{:S(2)}) %collective-permute-start.28) | collective-permute-done | bytes 262176 | tf_op jit(solution)/shard_map/ppermute | solution.py:919
  117.9 11.0 %all_to_all.10.refs_5_ = f32[8,2,8,128]{3,2,1,0:T(8,128)S(1)} all-to-all(f32[8,2,8,128]{3,2,1,0:T(8,128)S(1)} %broadcast_in_dim.89), channel_id=1, replica_groups=mesh['stream'=4,'batch'=8] {'batch'}, dimensions={0} | all-to-all | bytes 131072 | tf_op jit(solution)/shard_map/all_to_all | solution.py:1133
  130.3 9.7 %ffn_backward.1 = (f32[256,768]{1,0:T(8,128)}, f32[768,128]{1,0:T(8,128)}, f32[1,768]{1,0:T(1,128)}, bf16[2,2,256,1024]{3,2,1,0:T(8,128)(2,1)}, bf16[8,576,256]{...) custom-call(bf16[256,128]{1,0:T(8,128)(2,1)} %copy-done.8, ...), custom_call_target="tpu_custom_call" | custom-call | flops 3221225472 | bytes 27159552 | tf_op jit(solution)/shard_map/ffn_backward/pallas_call | solution.py:174
  139.9 4.0 %collective-permute-start.29 = (bf16[4,576,256]{2,1,0:T(8,128)(2,1)}, bf16[4,576,256]{2,1,0:T(8,128)(2,1)S(1)}, u32[]{:S(2)}, u32[]{:S(2)}) collective-permute-start(bf16[4,576,256]{2,1,0:T(8,128)(2,1)} %get-tuple-element.285), channel_id=1, source_target_pairs={{0,8},{1,9},{2,10},{3,11},{4,12},{5,13},{6,14},{7,15},{8,0},{9,1},... | collective-permute-start | bytes 3538952 | tf_op jit(solution)/shard_map/ppermute | solution.py:919
  144.0 2.6 %collective-permute-done.29.refs_1_ = bf16[4,576,256]{2,1,0:T(8,128)(2,1)S(1)} collective-permute-done((bf16[4,576,256]{2,1,0:T(8,128)(2,1)}, bf16[4,576,256]{2,1,0:T(8,128)(2,1)S(1)}, u32[]{:S(2)}, u32[]{:S(2)}) %collective-permute-start.29) | collective-permute-done | bytes 1179680 | tf_op jit(solution)/shard_map/ppermute | solution.py:919
  148.5 1.9 collective-permute-start.34
  150.4 8.5 %middle_backward.1 = (f32[256,768]{1,0:T(8,128)}, bf16[256,768]{1,0:T(8,128)(2,1)}, f32[1,768]{1,0:T(1,128)}) custom-call(f32[256,768]{1,0:T(8,128)} %get-tuple-element.283.refs_0_, f32[256,768]{1,0:T(8,128)} %get-tuple-element.262.refs_0_.refs_1_, bf16[2,2,256,1024]{3,2,1,0:T(8,128)(2,1)} %get-tuple-element.290.refs_2_, ...), custom_call_target="tpu_custom_call" | custom-call | flops 49999998976 | bytes 16673792 | tf_op jit(solution)/shard_map/middle_backward/pallas_call | solution.py:174
  158.9 2.5 base_up.3.refs_0_
  162.7 10.3 %attention_backward.1 = (f32[256,768]{1,0:T(8,128)}, bf16[2,208,768]{2,1,0:T(8,128)(2,1)}, bf16[6,208,768]{2,1,0:T(8,128)(2,1)}, bf16[2,208,768]{2,1,0:T(8,128)(2,1)}, bf16[6,208,768]{2,1,0:T(8,128)(2,1)}) custom-call(f32[256,768]{1,0:T(8,128)} %get-tuple-element.292.refs_0_, bf16[256,768]{1,0:T(8,128)(2,1)} %get-tuple-element.301.refs_1_, ...), custom_call_target="tpu_custom_call" | custom-call | flops 2113929216 | bytes 15398912 | tf_op jit(solution)/shard_map/attention_backward/pallas_call | solution.py:174
  173.5 2.4 base_up.5.refs_0_
  182.6 2.9 %base_up.4.refs_1_.refs_2_.refs_3_ = bf16[6,208,768]{2,1,0:T(8,128)(2,1)} custom-call(bf16[6,208,768]{2,1,0:T(8,128)(2,1)} %get-tuple-element.329.refs_0_, bf16[6,208,768]{2,1,0:T(8,128)(2,1)} %collective-permute-done.36.refs_1_), custom_call_target="tpu_custom_call" | custom-call | bytes 5750784 | tf_op jit(solution)/shard_map/base_up/pallas_call | solution.py:174
  185.5 7.8 %collective-permute-done.35.refs_2_ = bf16[2,576,256]{2,1,0:T(8,128)(2,1)} collective-permute-done((bf16[2,576,256]{2,1,0:T(8,128)(2,1)}, bf16[2,576,256]{2,1,0:T(8,128)(2,1)}, u32[]{:S(2)}, u32[]{:S(2)}) %collective-permute-start.35) | collective-permute-done | bytes 589856 | tf_op jit(solution)/shard_map/ppermute | solution.py:919
  194.7 12.3 %collective-permute-done.33.refs_0_ = bf16[2,208,768]{2,1,0:T(8,128)(2,1)} collective-permute-done((bf16[2,208,768]{2,1,0:T(8,128)(2,1)}, bf16[2,208,768]{2,1,0:T(8,128)(2,1)}, u32[]{:S(2)}, u32[]{:S(2)}) %collective-permute-start.33) | collective-permute-done | bytes 639008 | tf_op jit(solution)/shard_map/ppermute | solution.py:919
  207.0 1.7 add_up.17
  209.6 6.6 %collective-permute-done.39.refs_2_ = bf16[1,576,256]{2,1,0:T(8,128)(2,1)S(1)} collective-permute-done((bf16[1,576,256]{2,1,0:T(8,128)(2,1)S(1)}, bf16[1,576,256]{2,1,0:T(8,128)(2,1)S(1)}, u32[]{:S(2)}, u32[]{:S(2)}) %collective-permute-start.39) | collective-permute-done | bytes 294944 | tf_op jit(solution)/shard_map/ppermute | solution.py:919
  218.1 8.9 %collective-permute-done.37.refs_1_ = bf16[2,208,768]{2,1,0:T(8,128)(2,1)S(1)} collective-permute-done((bf16[2,208,768]{2,1,0:T(8,128)(2,1)S(1)}, bf16[2,208,768]{2,1,0:T(8,128)(2,1)S(1)}, u32[]{:S(2)}, u32[]{:S(2)}) %collective-permute-start.37) | collective-permute-done | bytes 639008 | tf_op jit(solution)/shard_map/ppermute | solution.py:919
  227.0 3.2 %collective-permute-done.41.refs_0_ = bf16[2,208,768]{2,1,0:T(8,128)(2,1)S(1)} collective-permute-done((bf16[2,208,768]{2,1,0:T(8,128)(2,1)S(1)}, bf16[2,208,768]{2,1,0:T(8,128)(2,1)S(1)}, u32[]{:S(2)}, u32[]{:S(2)}) %collective-permute-start.41) | collective-permute-done | bytes 639008 | tf_op jit(solution)/shard_map/ppermute | solution.py:919
  230.6 5.8 %collective-permute-done.43.refs_2_ = bf16[1,576,256]{2,1,0:T(8,128)(2,1)S(1)} collective-permute-done((bf16[1,576,256]{2,1,0:T(8,128)(2,1)S(1)}, bf16[1,576,256]{2,1,0:T(8,128)(2,1)S(1)}, u32[]{:S(2)}, u32[]{:S(2)}) %collective-permute-start.43) | collective-permute-done | bytes 294944 | tf_op jit(solution)/shard_map/ppermute | solution.py:919
  236.7 2.7 %collective-permute-start.46 = (bf16[1,576,256]{2,1,0:T(8,128)(2,1)S(1)}, bf16[1,576,256]{2,1,0:T(8,128)(2,1)S(1)}, u32[]{:S(2)}, u32[]{:S(2)}) collective-permute-start(bf16[1,576,256]{2,1,0:T(8,128)(2,1)S(1)} %add_up.21.refs_0_), channel_id=1, source_target_pairs={{0,16},{1,17},{2,18},{3,19},{4,20},{5,21},{6,22},{7,23},{8,24},{9,... | collective-permute-start | bytes 884744 | tf_op jit(solution)/shard_map/ppermute | solution.py:919
  239.4 2.9 %collective-permute-start.47 = (bf16[1,576,256]{2,1,0:T(8,128)(2,1)S(1)}, bf16[1,576,256]{2,1,0:T(8,128)(2,1)S(1)}, u32[]{:S(2)}, u32[]{:S(2)}) collective-permute-start(bf16[1,576,256]{2,1,0:T(8,128)(2,1)S(1)} %add_up.21.refs_0_), channel_id=1, source_target_pairs={{0,8},{1,9},{2,10},{3,11},{4,12},{5,13},{6,14},{7,15},{8,0},{9,1},... | collective-permute-start | bytes 884744 | tf_op jit(solution)/shard_map/ppermute | solution.py:919
  242.2 3.2 %collective-permute-done.42.refs_2_ = bf16[1,208,768]{2,1,0:T(8,128)(2,1)S(1)} collective-permute-done((bf16[1,208,768]{2,1,0:T(8,128)(2,1)S(1)}, bf16[1,208,768]{2,1,0:T(8,128)(2,1)S(1)}, u32[]{:S(2)}, u32[]{:S(2)}) %collective-permute-start.42) | collective-permute-done | bytes 319520 | tf_op jit(solution)/shard_map/ppermute | solution.py:919
  245.7 2.7 %collective-permute-start.45 = (bf16[1,208,768]{2,1,0:T(8,128)(2,1)S(1)}, bf16[1,208,768]{2,1,0:T(8,128)(2,1)S(1)}, u32[]{:S(2)}, u32[]{:S(2)}) collective-permute-start(bf16[1,208,768]{2,1,0:T(8,128)(2,1)S(1)} %add_up.22.refs_0_), channel_id=1, source_target_pairs={{0,16},{1,17},{2,18},{3,19},{4,20},{5,21},{6,22},{7,23},{8,24},{9,... | collective-permute-start | bytes 958472 | tf_op jit(solution)/shard_map/ppermute | solution.py:919
  248.4 2.7 %collective-permute-start.48 = (bf16[1,576,256]{2,1,0:T(8,128)(2,1)S(1)}, bf16[1,576,256]{2,1,0:T(8,128)(2,1)S(1)}, u32[]{:S(2)}, u32[]{:S(2)}) collective-permute-start(bf16[1,576,256]{2,1,0:T(8,128)(2,1)S(1)} %collective-permute-done.46.refs_1_), channel_id=1, source_target_pairs={{0,8},{1,9},{2,10},{3,11},{4,12},{5,13},{6,14},{7,15},{8,0},{9,1},... | collective-permute-start | bytes 884744 | tf_op jit(solution)/shard_map/ppermute | solution.py:919
  251.0 2.8 %collective-permute-done.45.refs_1_ = bf16[1,208,768]{2,1,0:T(8,128)(2,1)S(1)} collective-permute-done((bf16[1,208,768]{2,1,0:T(8,128)(2,1)S(1)}, bf16[1,208,768]{2,1,0:T(8,128)(2,1)S(1)}, u32[]{:S(2)}, u32[]{:S(2)}) %collective-permute-start.45) | collective-permute-done | bytes 319520 | tf_op jit(solution)/shard_map/ppermute | solution.py:919
  253.9 3.1 %collective-permute-start.49 = (bf16[1,208,768]{2,1,0:T(8,128)(2,1)S(1)}, bf16[1,208,768]{2,1,0:T(8,128)(2,1)S(1)}, u32[]{:S(2)}, u32[]{:S(2)}) collective-permute-start(bf16[1,208,768]{2,1,0:T(8,128)(2,1)S(1)} %add_up.23.refs_0_), channel_id=1, source_target_pairs={{0,8},{1,9},{2,10},{3,11},{4,12},{5,13},{6,14},{7,15},{8,0},{9,1},... | collective-permute-start | bytes 958472 | tf_op jit(solution)/shard_map/ppermute | solution.py:919
  257.0 1.6 finish_wide.1
  (171 shorter events, 52.5 us)
Async XLA Ops:
  3.3 20.2 %collective-permute-start = (bf16[1,576,256]{2,1,0:T(8,128)(2,1)}, bf16[1,576,256]{2,1,0:T(8,128)(2,1)}, u32[]{:S(2)}, u32[]{:S(2)}) collective-permute-start(bf16[1,576,256]{2,1,0:T(8,128)(2,1)} %bitcast.41), channel_id=1, source_target_pairs={{0,4},{1,5},{2,6},{3,7},{4,0},{5,1},{6,2},{7,3},{8,12},{9,13},{10,... | collective-permute-start | bytes 884744 | tf_op jit(solution)/shard_map/ppermute | solution.py:919
  6.5 17.0 %collective-permute-start.1 = (bf16[1,576,256]{2,1,0:T(8,128)(2,1)}, bf16[1,576,256]{2,1,0:T(8,128)(2,1)}, u32[]{:S(2)}, u32[]{:S(2)}) collective-permute-start(bf16[1,576,256]{2,1,0:T(8,128)(2,1)} %bitcast.42), channel_id=1, source_target_pairs={{0,2},{1,3},{2,0},{3,1},{4,6},{5,7},{6,4},{7,5},{8,10},{9,11},{10,... | collective-permute-start | bytes 884744 | tf_op jit(solution)/shard_map/ppermute | solution.py:919
  7.8 15.7 %collective-permute-start.2 = (bf16[1,576,256]{2,1,0:T(8,128)(2,1)}, bf16[1,576,256]{2,1,0:T(8,128)(2,1)}, u32[]{:S(2)}, u32[]{:S(2)}) collective-permute-start(bf16[1,576,256]{2,1,0:T(8,128)(2,1)} %bitcast.43), channel_id=1, source_target_pairs={{0,16},{1,17},{2,18},{3,19},{4,20},{5,21},{6,22},{7,23},{8,24},{9,... | collective-permute-start | bytes 884744 | tf_op jit(solution)/shard_map/ppermute | solution.py:919
  9.0 14.5 %collective-permute-start.3 = (bf16[1,576,256]{2,1,0:T(8,128)(2,1)}, bf16[1,576,256]{2,1,0:T(8,128)(2,1)}, u32[]{:S(2)}, u32[]{:S(2)}) collective-permute-start(bf16[1,576,256]{2,1,0:T(8,128)(2,1)} %bitcast.44), channel_id=1, source_target_pairs={{0,1},{1,0},{2,3},{3,2},{4,5},{5,4},{6,7},{7,6},{8,9},{9,8},{10,11... | collective-permute-start | bytes 884744 | tf_op jit(solution)/shard_map/ppermute | solution.py:919
  10.9 11.6 %all-to-all-start = ((s32[2,8,8,128]{3,2,0,1:T(8,128)}), s32[2,8,8,128]{3,2,0,1:T(8,128)S(1)}, u32[]{:S(2)}, u32[]{:S(2)}) async-start(s32[2,8,8,128]{3,2,0,1:T(8,128)} %copy.42), calls=%async_computation | async-start | bytes 131072 | tf_op jit(solution)/shard_map/all_to_all | solution.py:946
  14.2 10.5 %collective-permute-start.4 = (bf16[1,208,768]{2,1,0:T(8,128)(2,1)}, bf16[1,208,768]{2,1,0:T(8,128)(2,1)}, u32[]{:S(2)}, u32[]{:S(2)}) collective-permute-start(bf16[1,208,768]{2,1,0:T(8,128)(2,1)} %bitcast.37), channel_id=1, source_target_pairs={{0,1},{1,0},{2,3},{3,2},{4,5},{5,4},{6,7},{7,6},{8,9},{9,8},{10,11... | collective-permute-start | bytes 958472 | tf_op jit(solution)/shard_map/ppermute | solution.py:919
  24.8 25.0 %collective-permute-start.5 = (bf16[1,208,768]{2,1,0:T(8,128)(2,1)}, bf16[1,208,768]{2,1,0:T(8,128)(2,1)}, u32[]{:S(2)}, u32[]{:S(2)}) collective-permute-start(bf16[1,208,768]{2,1,0:T(8,128)(2,1)} %bitcast.38), channel_id=1, source_target_pairs={{0,2},{1,3},{2,0},{3,1},{4,6},{5,7},{6,4},{7,5},{8,10},{9,11},{10,... | collective-permute-start | bytes 958472 | tf_op jit(solution)/shard_map/ppermute | solution.py:919
  24.8 25.0 %collective-permute-start.9 = (bf16[1,208,768]{2,1,0:T(8,128)(2,1)}, bf16[1,208,768]{2,1,0:T(8,128)(2,1)}, u32[]{:S(2)}, u32[]{:S(2)}) collective-permute-start(bf16[1,208,768]{2,1,0:T(8,128)(2,1)} %bitcast.39), channel_id=1, source_target_pairs={{0,4},{1,5},{2,6},{3,7},{4,0},{5,1},{6,2},{7,3},{8,12},{9,13},{10,... | collective-permute-start | bytes 958472 | tf_op jit(solution)/shard_map/ppermute | solution.py:919
  26.7 20.0 %collective-permute-start.7 = (bf16[1,576,256]{2,1,0:T(8,128)(2,1)}, bf16[1,576,256]{2,1,0:T(8,128)(2,1)}, u32[]{:S(2)}, u32[]{:S(2)}) collective-permute-start(bf16[1,576,256]{2,1,0:T(8,128)(2,1)} %collective-permute-done), channel_id=1, source_target_pairs={{0,2},{1,3},{2,0},{3,1},{4,6},{5,7},{6,4},{7,5},{8,10},{9,11},{10,... | collective-permute-start | bytes 884744 | tf_op jit(solution)/shard_map/ppermute | solution.py:919
  31.4 15.3 %collective-permute-start.6 = (bf16[2,576,256]{2,1,0:T(8,128)(2,1)}, bf16[2,576,256]{2,1,0:T(8,128)(2,1)}, u32[]{:S(2)}, u32[]{:S(2)}) collective-permute-start(bf16[2,576,256]{2,1,0:T(8,128)(2,1)} %pad_maximum_fusion.4), channel_id=1, source_target_pairs={{0,1},{1,0},{2,3},{3,2},{4,5},{5,4},{6,7},{7,6},{8,9},{9,8},{10,11... | collective-permute-start | bytes 1769480 | tf_op jit(solution)/shard_map/ppermute | solution.py:919
  31.9 21.8 %collective-permute-start.12 = (bf16[3,576,256]{2,1,0:T(8,128)(2,1)}, bf16[3,576,256]{2,1,0:T(8,128)(2,1)}, u32[]{:S(2)}, u32[]{:S(2)}) collective-permute-start(bf16[3,576,256]{2,1,0:T(8,128)(2,1)} %pad_maximum_fusion.3), channel_id=1, source_target_pairs={{0,16},{1,17},{2,18},{3,19},{4,20},{5,21},{6,22},{7,23},{8,24},{9,... | collective-permute-start | bytes 2654216 | tf_op jit(solution)/shard_map/ppermute | solution.py:919
  47.7 7.4 %collective-permute-start.11 = (bf16[1,576,256]{2,1,0:T(8,128)(2,1)}, bf16[1,576,256]{2,1,0:T(8,128)(2,1)S(1)}, u32[]{:S(2)}, u32[]{:S(2)}) collective-permute-start(bf16[1,576,256]{2,1,0:T(8,128)(2,1)} %collective-permute-done.7), channel_id=1, source_target_pairs={{0,1},{1,0},{2,3},{3,2},{4,5},{5,4},{6,7},{7,6},{8,9},{9,8},{10,11... | collective-permute-start | bytes 884744 | tf_op jit(solution)/shard_map/ppermute | solution.py:919
  49.8 14.0 %collective-permute-start.14 = (bf16[1,208,768]{2,1,0:T(8,128)(2,1)}, bf16[1,208,768]{2,1,0:T(8,128)(2,1)}, u32[]{:S(2)}, u32[]{:S(2)}) collective-permute-start(bf16[1,208,768]{2,1,0:T(8,128)(2,1)} %collective-permute-done.9), channel_id=1, source_target_pairs={{0,2},{1,3},{2,0},{3,1},{4,6},{5,7},{6,4},{7,5},{8,10},{9,11},{10,... | collective-permute-start | bytes 958472 | tf_op jit(solution)/shard_map/ppermute | solution.py:919
  49.8 16.8 %collective-permute-start.10 = (bf16[1,208,768]{2,1,0:T(8,128)(2,1)}, bf16[1,208,768]{2,1,0:T(8,128)(2,1)}, u32[]{:S(2)}, u32[]{:S(2)}) collective-permute-start(bf16[1,208,768]{2,1,0:T(8,128)(2,1)} %collective-permute-done.9), channel_id=1, source_target_pairs={{0,1},{1,0},{2,3},{3,2},{4,5},{5,4},{6,7},{7,6},{8,9},{9,8},{10,11... | collective-permute-start | bytes 958472 | tf_op jit(solution)/shard_map/ppermute | solution.py:919
  50.5 18.4 %collective-permute-start.8 = (bf16[1,208,768]{2,1,0:T(8,128)(2,1)}, bf16[1,208,768]{2,1,0:T(8,128)(2,1)}, u32[]{:S(2)}, u32[]{:S(2)}) collective-permute-start(bf16[1,208,768]{2,1,0:T(8,128)(2,1)} %collective-permute-done.5), channel_id=1, source_target_pairs={{0,1},{1,0},{2,3},{3,2},{4,5},{5,4},{6,7},{7,6},{8,9},{9,8},{10,11... | collective-permute-start | bytes 958472 | tf_op jit(solution)/shard_map/ppermute | solution.py:919
  53.8 12.1 %collective-permute-start.16 = (bf16[2,576,256]{2,1,0:T(8,128)(2,1)S(1)}, bf16[2,576,256]{2,1,0:T(8,128)(2,1)}, u32[]{:S(2)}, u32[]{:S(2)}) collective-permute-start(bf16[2,576,256]{2,1,0:T(8,128)(2,1)S(1)} %pad_maximum_fusion.5), channel_id=1, source_target_pairs={{0,16},{1,17},{2,18},{3,19},{4,20},{5,21},{6,22},{7,23},{8,24},{9,... | collective-permute-start | bytes 1769480 | tf_op jit(solution)/shard_map/ppermute | solution.py:919
  57.1 16.0 %collective-permute-start.13 = (bf16[8,576,256]{2,1,0:T(8,128)(2,1)S(1)}, bf16[8,576,256]{2,1,0:T(8,128)(2,1)}, u32[]{:S(2)}, u32[]{:S(2)}) collective-permute-start(bf16[8,576,256]{2,1,0:T(8,128)(2,1)S(1)} %constant_dynamic-update-slice_fusion.refs_4_.refs_9_), channel_id=1, source_target_pairs={{0,8},{1,9},{2,10},{3,11},{4,12},{5,13},{6,14},{7,15},{8,0},{9,1},... | collective-permute-start | bytes 7077896 | tf_op jit(solution)/shard_map/ppermute | solution.py:919
  63.8 9.3 %collective-permute-start.15 = (bf16[4,208,768]{2,1,0:T(8,128)(2,1)}, bf16[4,208,768]{2,1,0:T(8,128)(2,1)}, u32[]{:S(2)}, u32[]{:S(2)}) collective-permute-start(bf16[4,208,768]{2,1,0:T(8,128)(2,1)} %pad_maximum_fusion.refs_3_), channel_id=1, source_target_pairs={{0,8},{1,9},{2,10},{3,11},{4,12},{5,13},{6,14},{7,15},{8,0},{9,1},... | collective-permute-start | bytes 3833864 | tf_op jit(solution)/shard_map/ppermute | solution.py:919
  65.9 9.5 %collective-permute-start.21 = (bf16[1,208,768]{2,1,0:T(8,128)(2,1)}, bf16[1,208,768]{2,1,0:T(8,128)(2,1)}, u32[]{:S(2)}, u32[]{:S(2)}) collective-permute-start(bf16[1,208,768]{2,1,0:T(8,128)(2,1)} %collective-permute-done.14), channel_id=1, source_target_pairs={{0,1},{1,0},{2,3},{3,2},{4,5},{5,4},{6,7},{7,6},{8,9},{9,8},{10,11... | collective-permute-start | bytes 958472 | tf_op jit(solution)/shard_map/ppermute | solution.py:919
  66.7 11.9 %collective-permute-start.19 = (bf16[2,576,256]{2,1,0:T(8,128)(2,1)}, bf16[2,576,256]{2,1,0:T(8,128)(2,1)}, u32[]{:S(2)}, u32[]{:S(2)}) collective-permute-start(bf16[2,576,256]{2,1,0:T(8,128)(2,1)} %pad_maximum_fusion.6), channel_id=1, source_target_pairs={{0,16},{1,17},{2,18},{3,19},{4,20},{5,21},{6,22},{7,23},{8,24},{9,... | collective-permute-start | bytes 1769480 | tf_op jit(solution)/shard_map/ppermute | solution.py:919
  68.8 21.2 %collective-permute-start.18 = (bf16[2,576,256]{2,1,0:T(8,128)(2,1)}, bf16[2,576,256]{2,1,0:T(8,128)(2,1)}, u32[]{:S(2)}, u32[]{:S(2)}) collective-permute-start(bf16[2,576,256]{2,1,0:T(8,128)(2,1)} %collective-permute-done.16.refs_7_.refs_12_), channel_id=1, source_target_pairs={{0,8},{1,9},{2,10},{3,11},{4,12},{5,13},{6,14},{7,15},{8,0},{9,1},... | collective-permute-start | bytes 1769480 | tf_op jit(solution)/shard_map/ppermute | solution.py:919
  75.3 4.6 %collective-permute-start.22 = (bf16[1,208,768]{2,1,0:T(8,128)(2,1)}, bf16[1,208,768]{2,1,0:T(8,128)(2,1)S(1)}, u32[]{:S(2)}, u32[]{:S(2)}) collective-permute-start(bf16[1,208,768]{2,1,0:T(8,128)(2,1)} %collective-permute-done.21.refs_5_), channel_id=1, source_target_pairs={{0,8},{1,9},{2,10},{3,11},{4,12},{5,13},{6,14},{7,15},{8,0},{9,1},... | collective-permute-start | bytes 958472 | tf_op jit(solution)/shard_map/ppermute | solution.py:919
  78.1 11.9 %collective-permute-start.17 = (bf16[4,576,256]{2,1,0:T(8,128)(2,1)}, bf16[4,576,256]{2,1,0:T(8,128)(2,1)S(1)}, u32[]{:S(2)}, u32[]{:S(2)}) collective-permute-start(bf16[4,576,256]{2,1,0:T(8,128)(2,1)} %pad_maximum_fusion.1.refs_6_.refs_11_), channel_id=1, source_target_pairs={{0,8},{1,9},{2,10},{3,11},{4,12},{5,13},{6,14},{7,15},{8,0},{9,1},... | collective-permute-start | bytes 3538952 | tf_op jit(solution)/shard_map/ppermute | solution.py:919
  82.1 8.0 %collective-permute-start.23 = (bf16[2,576,256]{2,1,0:T(8,128)(2,1)}, bf16[2,576,256]{2,1,0:T(8,128)(2,1)S(1)}, u32[]{:S(2)}, u32[]{:S(2)}) collective-permute-start(bf16[2,576,256]{2,1,0:T(8,128)(2,1)} %collective-permute-done.19.refs_8_.refs_13_), channel_id=1, source_target_pairs={{0,8},{1,9},{2,10},{3,11},{4,12},{5,13},{6,14},{7,15},{8,0},{9,1},... | collective-permute-start | bytes 1769480 | tf_op jit(solution)/shard_map/ppermute | solution.py:919
  100.5 5.7 %collective-permute-start.24 = (bf16[256,128]{1,0:T(8,128)(2,1)}, bf16[256,128]{1,0:T(8,128)(2,1)S(1)}, u32[]{:S(2)}, u32[]{:S(2)}) collective-permute-start(bf16[256,128]{1,0:T(8,128)(2,1)} %get-tuple-element.271.refs_0_), channel_id=1, source_target_pairs={{0,16},{1,17},{2,18},{3,19},{4,20},{5,21},{6,22},{7,23},{8,24},{9,... | collective-permute-start | bytes 196616 | tf_op jit(solution)/shard_map/ppermute | solution.py:919
  100.5 5.6 %collective-permute-start.25 = (bf16[256,128]{1,0:T(8,128)(2,1)}, bf16[256,128]{1,0:T(8,128)(2,1)S(1)}, u32[]{:S(2)}, u32[]{:S(2)}) collective-permute-start(bf16[256,128]{1,0:T(8,128)(2,1)} %get-tuple-element.271.refs_0_), channel_id=1, source_target_pairs={{0,18},{1,19},{2,16},{3,17},{4,22},{5,23},{6,20},{7,21},{8,26},{9,... | collective-permute-start | bytes 196616 | tf_op jit(solution)/shard_map/ppermute | solution.py:919
  103.1 5.6 %collective-permute-start.26 = (bf16[256,128]{1,0:T(8,128)(2,1)}, bf16[256,128]{1,0:T(8,128)(2,1)S(1)}, u32[]{:S(2)}, u32[]{:S(2)}) collective-permute-start(bf16[256,128]{1,0:T(8,128)(2,1)} %get-tuple-element.271.refs_0_), channel_id=1, source_target_pairs={{0,20},{1,21},{2,22},{3,23},{4,16},{5,17},{6,18},{7,19},{8,28},{9,... | collective-permute-start | bytes 196616 | tf_op jit(solution)/shard_map/ppermute | solution.py:919
  104.5 6.0 %collective-permute-start.27 = (bf16[256,128]{1,0:T(8,128)(2,1)}, bf16[256,128]{1,0:T(8,128)(2,1)S(1)}, u32[]{:S(2)}, u32[]{:S(2)}) collective-permute-start(bf16[256,128]{1,0:T(8,128)(2,1)} %get-tuple-element.271.refs_0_), channel_id=1, source_target_pairs={{0,22},{1,23},{2,20},{3,21},{4,18},{5,19},{6,16},{7,17},{8,30},{9,... | collective-permute-start | bytes 196616 | tf_op jit(solution)/shard_map/ppermute | solution.py:919
  110.6 5.3 %collective-permute-start.28 = (bf16[4,256,128]{2,1,0:T(8,128)(2,1)S(1)}, bf16[4,256,128]{2,1,0:T(8,128)(2,1)S(1)}, u32[]{:S(2)}, u32[]{:S(2)}) collective-permute-start(bf16[4,256,128]{2,1,0:T(8,128)(2,1)S(1)} %pad_maximum_fusion.7.refs_3_.refs_6_), channel_id=1, source_target_pairs={{0,1},{1,0},{2,3},{3,2},{4,5},{5,4},{6,7},{7,6},{8,9},{9,8},{10,11... | collective-permute-start | bytes 786440 | tf_op jit(solution)/shard_map/ppermute | solution.py:919
  139.9 6.6 %collective-permute-start.29 = (bf16[4,576,256]{2,1,0:T(8,128)(2,1)}, bf16[4,576,256]{2,1,0:T(8,128)(2,1)S(1)}, u32[]{:S(2)}, u32[]{:S(2)}) collective-permute-start(bf16[4,576,256]{2,1,0:T(8,128)(2,1)} %get-tuple-element.285), channel_id=1, source_target_pairs={{0,8},{1,9},{2,10},{3,11},{4,12},{5,13},{6,14},{7,15},{8,0},{9,1},... | collective-permute-start | bytes 3538952 | tf_op jit(solution)/shard_map/ppermute | solution.py:919
  143.9 15.0 %collective-permute-start.30 = (bf16[4,576,256]{2,1,0:T(8,128)(2,1)}, bf16[4,576,256]{2,1,0:T(8,128)(2,1)S(1)}, u32[]{:S(2)}, u32[]{:S(2)}) collective-permute-start(bf16[4,576,256]{2,1,0:T(8,128)(2,1)} %get-tuple-element.294), channel_id=1, source_target_pairs={{0,8},{1,9},{2,10},{3,11},{4,12},{5,13},{6,14},{7,15},{8,0},{9,1},... | collective-permute-start | bytes 3538952 | tf_op jit(solution)/shard_map/ppermute | solution.py:919
  146.6 12.3 %collective-permute-start.31 = (bf16[8,576,256]{2,1,0:T(8,128)(2,1)}, bf16[8,576,256]{2,1,0:T(8,128)(2,1)}, u32[]{:S(2)}, u32[]{:S(2)}) collective-permute-start(bf16[8,576,256]{2,1,0:T(8,128)(2,1)} %get-tuple-element.295), channel_id=1, source_target_pairs={{0,8},{1,9},{2,10},{3,11},{4,12},{5,13},{6,14},{7,15},{8,0},{9,1},... | collective-permute-start | bytes 7077896 | tf_op jit(solution)/shard_map/ppermute | solution.py:919
  148.5 28.4 %collective-permute-start.34 = (bf16[4,576,256]{2,1,0:T(8,128)(2,1)S(1)}, bf16[4,576,256]{2,1,0:T(8,128)(2,1)S(1)}, u32[]{:S(2)}, u32[]{:S(2)}) collective-permute-start(bf16[4,576,256]{2,1,0:T(8,128)(2,1)S(1)} %add_up.12), channel_id=1, source_target_pairs={{0,16},{1,17},{2,18},{3,19},{4,20},{5,21},{6,22},{7,23},{8,24},{9,... | collective-permute-start | bytes 3538952 | tf_op jit(solution)/shard_map/ppermute | solution.py:919
  178.5 14.8 %collective-permute-start.35 = (bf16[2,576,256]{2,1,0:T(8,128)(2,1)}, bf16[2,576,256]{2,1,0:T(8,128)(2,1)}, u32[]{:S(2)}, u32[]{:S(2)}) collective-permute-start(bf16[2,576,256]{2,1,0:T(8,128)(2,1)} %add_up.15), channel_id=1, source_target_pairs={{0,1},{1,0},{2,3},{3,2},{4,5},{5,4},{6,7},{7,6},{8,9},{9,8},{10,11... | collective-permute-start | bytes 1769480 | tf_op jit(solution)/shard_map/ppermute | solution.py:919
  178.6 28.4 %collective-permute-start.33 = (bf16[2,208,768]{2,1,0:T(8,128)(2,1)}, bf16[2,208,768]{2,1,0:T(8,128)(2,1)}, u32[]{:S(2)}, u32[]{:S(2)}) collective-permute-start(bf16[2,208,768]{2,1,0:T(8,128)(2,1)} %add_up.14), channel_id=1, source_target_pairs={{0,1},{1,0},{2,3},{3,2},{4,5},{5,4},{6,7},{7,6},{8,9},{9,8},{10,11... | collective-permute-start | bytes 1916936 | tf_op jit(solution)/shard_map/ppermute | solution.py:919
  180.0 28.7 %collective-permute-start.38 = (bf16[4,576,256]{2,1,0:T(8,128)(2,1)}, bf16[4,576,256]{2,1,0:T(8,128)(2,1)S(1)}, u32[]{:S(2)}, u32[]{:S(2)}) collective-permute-start(bf16[4,576,256]{2,1,0:T(8,128)(2,1)} %add_up.13), channel_id=1, source_target_pairs={{0,16},{1,17},{2,18},{3,19},{4,20},{5,21},{6,22},{7,23},{8,24},{9,... | collective-permute-start | bytes 3538952 | tf_op jit(solution)/shard_map/ppermute | solution.py:919
  194.6 21.6 %collective-permute-start.40 = (bf16[2,576,256]{2,1,0:T(8,128)(2,1)S(1)}, bf16[2,576,256]{2,1,0:T(8,128)(2,1)S(1)}, u32[]{:S(2)}, u32[]{:S(2)}) collective-permute-start(bf16[2,576,256]{2,1,0:T(8,128)(2,1)S(1)} %add_up.16), channel_id=1, source_target_pairs={{0,2},{1,3},{2,0},{3,1},{4,6},{5,7},{6,4},{7,5},{8,10},{9,11},{10,... | collective-permute-start | bytes 1769480 | tf_op jit(solution)/shard_map/ppermute | solution.py:919
  208.9 7.3 %collective-permute-start.39 = (bf16[1,576,256]{2,1,0:T(8,128)(2,1)S(1)}, bf16[1,576,256]{2,1,0:T(8,128)(2,1)S(1)}, u32[]{:S(2)}, u32[]{:S(2)}) collective-permute-start(bf16[1,576,256]{2,1,0:T(8,128)(2,1)S(1)} %get-tuple-element.348), channel_id=1, source_target_pairs={{0,1},{1,0},{2,3},{3,2},{4,5},{5,4},{6,7},{7,6},{8,9},{9,8},{10,11... | collective-permute-start | bytes 884744 | tf_op jit(solution)/shard_map/ppermute | solution.py:919
  209.0 18.0 %collective-permute-start.37 = (bf16[2,208,768]{2,1,0:T(8,128)(2,1)S(1)}, bf16[2,208,768]{2,1,0:T(8,128)(2,1)S(1)}, u32[]{:S(2)}, u32[]{:S(2)}) collective-permute-start(bf16[2,208,768]{2,1,0:T(8,128)(2,1)S(1)} %get-tuple-element.341), channel_id=1, source_target_pairs={{0,2},{1,3},{2,0},{3,1},{4,6},{5,7},{6,4},{7,5},{8,10},{9,11},{10,... | collective-permute-start | bytes 1916936 | tf_op jit(solution)/shard_map/ppermute | solution.py:919
  216.4 13.8 %collective-permute-start.41 = (bf16[2,208,768]{2,1,0:T(8,128)(2,1)S(1)}, bf16[2,208,768]{2,1,0:T(8,128)(2,1)S(1)}, u32[]{:S(2)}, u32[]{:S(2)}) collective-permute-start(bf16[2,208,768]{2,1,0:T(8,128)(2,1)S(1)} %get-tuple-element.356), channel_id=1, source_target_pairs={{0,1},{1,0},{2,3},{3,2},{4,5},{5,4},{6,7},{7,6},{8,9},{9,8},{10,11... | collective-permute-start | bytes 1916936 | tf_op jit(solution)/shard_map/ppermute | solution.py:919
  216.5 20.0 %collective-permute-start.43 = (bf16[1,576,256]{2,1,0:T(8,128)(2,1)S(1)}, bf16[1,576,256]{2,1,0:T(8,128)(2,1)S(1)}, u32[]{:S(2)}, u32[]{:S(2)}) collective-permute-start(bf16[1,576,256]{2,1,0:T(8,128)(2,1)S(1)} %get-tuple-element.362), channel_id=1, source_target_pairs={{0,1},{1,0},{2,3},{3,2},{4,5},{5,4},{6,7},{7,6},{8,9},{9,8},{10,11... | collective-permute-start | bytes 884744 | tf_op jit(solution)/shard_map/ppermute | solution.py:919
  217.9 18.6 %collective-permute-start.44 = (bf16[1,576,256]{2,1,0:T(8,128)(2,1)S(1)}, bf16[1,576,256]{2,1,0:T(8,128)(2,1)S(1)}, u32[]{:S(2)}, u32[]{:S(2)}) collective-permute-start(bf16[1,576,256]{2,1,0:T(8,128)(2,1)S(1)} %add_up.19), channel_id=1, source_target_pairs={{0,4},{1,5},{2,6},{3,7},{4,0},{5,1},{6,2},{7,3},{8,12},{9,13},{10,... | collective-permute-start | bytes 884744 | tf_op jit(solution)/shard_map/ppermute | solution.py:919
  230.4 15.1 %collective-permute-start.42 = (bf16[1,208,768]{2,1,0:T(8,128)(2,1)S(1)}, bf16[1,208,768]{2,1,0:T(8,128)(2,1)S(1)}, u32[]{:S(2)}, u32[]{:S(2)}) collective-permute-start(bf16[1,208,768]{2,1,0:T(8,128)(2,1)S(1)} %add_up.20), channel_id=1, source_target_pairs={{0,4},{1,5},{2,6},{3,7},{4,0},{5,1},{6,2},{7,3},{8,12},{9,13},{10,... | collective-permute-start | bytes 958472 | tf_op jit(solution)/shard_map/ppermute | solution.py:919
  236.7 11.7 %collective-permute-start.46 = (bf16[1,576,256]{2,1,0:T(8,128)(2,1)S(1)}, bf16[1,576,256]{2,1,0:T(8,128)(2,1)S(1)}, u32[]{:S(2)}, u32[]{:S(2)}) collective-permute-start(bf16[1,576,256]{2,1,0:T(8,128)(2,1)S(1)} %add_up.21.refs_0_), channel_id=1, source_target_pairs={{0,16},{1,17},{2,18},{3,19},{4,20},{5,21},{6,22},{7,23},{8,24},{9,... | collective-permute-start | bytes 884744 | tf_op jit(solution)/shard_map/ppermute | solution.py:919
  239.4 9.0 %collective-permute-start.47 = (bf16[1,576,256]{2,1,0:T(8,128)(2,1)S(1)}, bf16[1,576,256]{2,1,0:T(8,128)(2,1)S(1)}, u32[]{:S(2)}, u32[]{:S(2)}) collective-permute-start(bf16[1,576,256]{2,1,0:T(8,128)(2,1)S(1)} %add_up.21.refs_0_), channel_id=1, source_target_pairs={{0,8},{1,9},{2,10},{3,11},{4,12},{5,13},{6,14},{7,15},{8,0},{9,1},... | collective-permute-start | bytes 884744 | tf_op jit(solution)/shard_map/ppermute | solution.py:919
  245.7 8.1 %collective-permute-start.45 = (bf16[1,208,768]{2,1,0:T(8,128)(2,1)S(1)}, bf16[1,208,768]{2,1,0:T(8,128)(2,1)S(1)}, u32[]{:S(2)}, u32[]{:S(2)}) collective-permute-start(bf16[1,208,768]{2,1,0:T(8,128)(2,1)S(1)} %add_up.22.refs_0_), channel_id=1, source_target_pairs={{0,16},{1,17},{2,18},{3,19},{4,20},{5,21},{6,22},{7,23},{8,24},{9,... | collective-permute-start | bytes 958472 | tf_op jit(solution)/shard_map/ppermute | solution.py:919
  248.4 5.5 %collective-permute-start.48 = (bf16[1,576,256]{2,1,0:T(8,128)(2,1)S(1)}, bf16[1,576,256]{2,1,0:T(8,128)(2,1)S(1)}, u32[]{:S(2)}, u32[]{:S(2)}) collective-permute-start(bf16[1,576,256]{2,1,0:T(8,128)(2,1)S(1)} %collective-permute-done.46.refs_1_), channel_id=1, source_target_pairs={{0,8},{1,9},{2,10},{3,11},{4,12},{5,13},{6,14},{7,15},{8,0},{9,1},... | collective-permute-start | bytes 884744 | tf_op jit(solution)/shard_map/ppermute | solution.py:919
  253.9 4.6 %collective-permute-start.49 = (bf16[1,208,768]{2,1,0:T(8,128)(2,1)S(1)}, bf16[1,208,768]{2,1,0:T(8,128)(2,1)S(1)}, u32[]{:S(2)}, u32[]{:S(2)}) collective-permute-start(bf16[1,208,768]{2,1,0:T(8,128)(2,1)S(1)} %add_up.23.refs_0_), channel_id=1, source_target_pairs={{0,8},{1,9},{2,10},{3,11},{4,12},{5,13},{6,14},{7,15},{8,0},{9,1},... | collective-permute-start | bytes 958472 | tf_op jit(solution)/shard_map/ppermute | solution.py:919
  (23 other events, 182.9 us)
where the time goes:
time: 261 us; the launch traced here: 260 us
  waiting for transfers between devices  89.6 us (34%)
  Pallas kernels  68.2 us (26%)
  starting transfers between devices  65.2 us (25%)
  other arithmetic  12.9 us (5%)
  local copies, waits for them, and re-layouts  11.5 us (4%)
  blocking collectives  11 us (4%)
    ppermute x50, waiting for transfers between devices, swap(): return lax.ppermute(block, EVERY, route)  86 us
    pallas_call x26, Pallas kernels, call(): pl.pallas_call(body, name=name, out_shape=shapes, in_specs=[kind] * len(a...  68.2 us
    ppermute x50, starting transfers between devices, swap(): return lax.ppermute(block, EVERY, route)  61.9 us
    concatenate x7, other arithmetic, join(): return jnp.concatenate(parts)  12.1 us
    all_to_all x1, blocking collectives, local(): lax.all_to_all(blocks, 'batch', split_axis=0, concat_axis=0, tiled=True)  11 us
    unnamed x45, local copies, waits for them, and re-layouts  7.79 us
  transfers between devices with their start and end apart: 51, of which 22 were waited for; matrix products, arithmetic and copies ran while one was open for 8% of the time, Pallas kernels for 16%

commit v1 on v0

--- a/solution.py
+++ b/solution.py
@@ -285,34 +285,48 @@
     )
 
 
-def pack_kernel(ids, wq, wk, wv, wo, wg, wu, wd, wp, g1, g2, g3, table, slab_a, slab_f):
-    y, core = ids[1], ids[2]
+def pack_kernel(ids, g1, g2, g3, table, wq, wk, wv, wo, wg, wu, wd, wp, slab_a, slab_f, sems):
+    y, core, ready, send = ids[1], ids[2], ids[4], ids[5]
 
     def fill(top, bottom, wide, rank):
-        slab_a[0:96, :] = top[...]
-        slab_a[96:192, :] = bottom[...]
         for yy in range(2):
 
             @pl.when(y == yy)
             def _():
+                pairs = []
                 for k in range(4):
-                    start = yy * HALF + k * 256
-                    slab_f[k * 96 : (k + 1) * 96, :] = wide[:, start : start + 256]
-                row = (2 * yy + rank) * 64
+                    lanes = pl.ds(yy * HALF + k * 256, 256)
+                    pairs.append((wide.at[:, lanes], slab_f.at[pl.ds(k * 96, 96)]))
+                rows = pl.ds((2 * yy + rank) * 64, 64)
                 for k in range(3):
-                    slab_f[384 + k * 64 : 384 + (k + 1) * 64, :] = wd[
-                        row : row + 64, k * 256 : (k + 1) * 256
-                    ]
+                    part = wd.at[rows, pl.ds(k * 256, 256)]
+                    pairs.append((part, slab_f.at[pl.ds(384 + k * 64, 64)]))
+                copies(pairs, sems.at[0])
+
+        pairs = [(top, slab_a.at[pl.ds(0, 96)]), (bottom, slab_a.at[pl.ds(96, 96)])]
+        copies(pairs, sems.at[1])
 
     @pl.when(core == 0)
     def _():
         fill(wq, wv, wg, 0)
         for k in range(6):
-            slab_a[192:208, k * DLEN : (k + 1) * DLEN] = wp[k * 16 : (k + 1) * 16, :]
+            place = slab_a.at[pl.ds(192, 16), pl.ds(k * DLEN, DLEN)]
+            copies([(wp.at[pl.ds(k * 16, 16)], place)], sems.at[1])
 
     @pl.when(core == 1)
     def _():
         fill(wk, wo, wu, 1)
+
+    ready()
+    landed(slab_f, sems.at[0])
+    send(1)
+
+    @pl.when(core == 0)
+    def _():
+        landed(slab_a, sems.at[1])
+
+    @pl.when(core == 1)
+    def _():
         rows = [g1[...].astype(F32), g2[...].astype(F32), g3[...].astype(F32)]
         head = jnp.concatenate(rows + [jnp.zeros((5, 96), F32)], axis=0)
         tail = jnp.concatenate([table[...].astype(F32), jnp.zeros((7, 48), F32)], axis=0)
@@ -321,6 +335,7 @@
         slab_a[192:208, :] = jnp.concatenate(
             [both, jnp.zeros((16, D - 96), F32)], axis=1
         ).astype(BF)
+        landed(slab_a.at[pl.ds(0, 192)], sems.at[1])
 
 
 def copies(pairs, sem):
@@ -545,7 +560,7 @@
         j = (b ^ m) if direct else m
         for micro in range(MICRO):
             rows = slice(micro * DLEN, (micro + 1) * DLEN)
-            mine, theirs = own[rows, :], block_of(others, m)[rows, :]
+            mine, theirs = own[0, rows, :], block_of(others, m)[rows, :]
             doc = jnp.where(is_query == 1, theirs, mine)
             query = jnp.where(is_query == 1, mine, theirs)
             times = counts[micro, j]
@@ -855,23 +870,27 @@
 
 
 def finish_narrow_kernel(
-    ids, near, twin, grad_q, grad_k, grad_v, grad_o, grad_p, grad_1, grad_2, grad_3, table
+    ids, near, near_far, twin, twin_far, grad_q, grad_k, grad_v, grad_o, grad_p, grad_1, grad_2, grad_3, table
 ):
     core = ids[2]
     for c in range(2):
 
         @pl.when(core == c)
         def _():
-            low, high = (twin, near) if c else (near, twin)
-            grad_q[...] = low[0, 0:96, :].astype(F32)
-            grad_k[...] = high[0, 0:96, :].astype(F32)
-            grad_v[...] = low[0, 96:192, :].astype(F32)
-            grad_o[...] = high[0, 96:192, :].astype(F32)
+            pairs = [(near, near_far), (twin, twin_far)]
+            low, high = pairs[::-1] if c else pairs
+
+            def summed(pair, rows):
+                return pair[0][0, rows, :].astype(F32) + pair[1][0, rows, :].astype(F32)
+
+            grad_q[...] = summed(low, slice(0, 96))
+            grad_k[...] = summed(high, slice(0, 96))
+            grad_v[...] = summed(low, slice(96, 192))
+            grad_o[...] = summed(high, slice(96, 192))
+            packed = summed(low, slice(192, 208))
             for k in range(6):
-                grad_p[k * 16 : (k + 1) * 16, :] = low[
-                    0, 192:208, k * DLEN : (k + 1) * DLEN
-                ].astype(F32)
-            rows = high[0, 192:208, :].astype(F32)
+                grad_p[k * 16 : (k + 1) * 16, :] = packed[:, k * DLEN : (k + 1) * DLEN]
+            rows = summed(high, slice(192, 208))
             grad_1[...] = rows[0:1, :96]
             grad_2[...] = rows[1:2, :96]
             grad_3[...] = rows[2:3, :96]
@@ -961,8 +980,11 @@
         slab_a, slab_f = call(
             pack_kernel,
             "pack",
-            [w_query, w_key, w_value, w_out, w_gate, w_up, w_down, w_proj, *lines],
+            lines,
             [((PIECE_A, D), BF), ((PIECE_F, 256), BF)],
+            far=[w_query, w_key, w_value, w_out, w_gate, w_up, w_down, w_proj],
+            sems=2,
+            lazy=True,
         )
 
         def join(*parts):
@@ -1112,7 +1134,9 @@
 
     if direct:
         even = jnp.stack([swap(vectors, 1, 0, m) for m in (0, 2, 4, 6)])
-        others = [even, swap(even, 0, 0, 1)]
+        odd = swap(even, 0, 0, 1)
+        own, odd = fence((jnp.stack([vectors, vectors]), odd))
+        others = [even, odd]
     else:
         route = [(i, (i + pairs) % streams) for i in range(streams)]
         arrived = lax.ppermute(vectors, "stream", route)
@@ -1122,7 +1146,7 @@
     soft, score = call(
         functools.partial(similarity_kernel, direct, shards),
         "similarity",
-        [vectors, counts, share, *others],
+        [own if direct else vectors[None], counts, share, *others],
         [block_f32, line_f32],
         [line_f32],
         limit=small,
@@ -1279,14 +1303,12 @@
         za4, token = fence((za4, token))
         (part_a,) = add_up([own_a(0, (xa51, 1), (za62, 1), (za4, 0))])
         part_a, token = fence((part_a, token))
-        ya = along_y(part_a)
+        ya, twin_part = along_y(part_a), other_core(part_a)
 
         far, twin_f, token = fence((far, twin_f, token))
         far_twin_f = other_core(far)
-        ya, token = fence((ya, token))
-        (mine_a,) = add_up([[(part_a, 0), (ya, 0)]])
-        mine_a, far_twin_f, token = fence((mine_a, far_twin_f, token))
-        twin_a = other_core(mine_a)
+        ya, far_twin_f, twin_part, token = fence((ya, far_twin_f, twin_part, token))
+        twin_ya = other_core(ya)
         shard_f32, wide_f32 = ((96, D), F32), ((96, FF), F32)
         grad_g, grad_u, grad_d = call(
             finish_wide_kernel,
@@ -1300,7 +1322,7 @@
         grad_q, grad_k, grad_v, grad_o, grad_p, *small = call(
             finish_narrow_kernel,
             "finish_narrow",
-            [mine_a, twin_a],
+            [part_a, ya, twin_part, twin_ya],
             [shard_f32] * 4 + [((96, DLEN), F32), ((1, 96), F32), ((1, 96), F32), ((1, 96), F32)]
             + [((1, 48), F32)],
             limit=24,

time: 261 us -> 259 us (level)
    ppermute x50 -> x51, waiting for transfers between devices: 86 us -> 85 us  [swap(): return lax.ppermute(block, EVERY, route)]
    unnamed x45 -> x43, local copies, waits for them, and re-layouts: 7.79 us -> 6.95 us
    pallas_call x26 -> x25, Pallas kernels: 68.2 us -> 67.7 us  [call(): pl.pallas_call(body, name=name, out_shape=shapes, in_specs=[kind] * len(a...]
    ppermute x50 -> x51, starting transfers between devices: 61.9 us -> 61.8 us  [swap(): return lax.ppermute(block, EVERY, route)]
  transfers between devices with their start and end apart: 51 -> 52, of which waited for: 22 -> 23; matrix products, arithmetic and copies ran while one was open for 8% -> 8% of each run, Pallas kernels for 16% -> 17%
where the time goes in v1:
time: 259 us; the launch traced here: 258 us
  waiting for transfers between devices  88.7 us (34%)
  Pallas kernels  67.7 us (26%)
  starting transfers between devices  65.1 us (25%)
  other arithmetic  13.9 us (5%)
  blocking collectives  10.9 us (4%)
  local copies, waits for them, and re-layouts  10.6 us (4%)
    ppermute x51, waiting for transfers between devices, swap(): return lax.ppermute(block, EVERY, route)  85 us
    pallas_call x25, Pallas kernels, call(): pl.pallas_call(body, name=name, out_shape=shapes, in_specs=[kind] * len(a...  67.7 us
    ppermute x51, starting transfers between devices, swap(): return lax.ppermute(block, EVERY, route)  61.8 us
    concatenate x7, other arithmetic, join(): return jnp.concatenate(parts)  12.1 us
    all_to_all x1, blocking collectives, local(): lax.all_to_all(blocks, 'batch', split_axis=0, concat_axis=0, tiled=True)  10.9 us
    unnamed x43, local copies, waits for them, and re-layouts  6.95 us
  transfers between devices with their start and end apart: 52, of which 23 were waited for; matrix products, arithmetic and copies ran while one was open for 8% of the time, Pallas kernels for 17%

profile of v1, /device:TPU:1, one launch (start us, length us, event | category | flops | bytes accessed | tf_op | source)
XLA Modules:
  0.0 258.3 jit_solution(7364454454679762737)
XLA Ops:
  0.7 2.0 pack.1
  2.7 3.2 %collective-permute-start = (bf16[1,576,256]{2,1,0:T(8,128)(2,1)}, bf16[1,576,256]{2,1,0:T(8,128)(2,1)}, u32[]{:S(2)}, u32[]{:S(2)}) collective-permute-start(bf16[1,576,256]{2,1,0:T(8,128)(2,1)} %bitcast.41), channel_id=1, source_target_pairs={{0,4},{1,5},{2,6},{3,7},{4,0},{5,1},{6,2},{7,3},{8,12},{9,13},{10,... | collective-permute-start | bytes 884744 | tf_op jit(solution)/shard_map/ppermute | solution.py:938
  10.3 3.4 %all-to-all-start = ((s32[2,8,8,128]{3,2,0,1:T(8,128)}), s32[2,8,8,128]{3,2,0,1:T(8,128)S(1)}, u32[]{:S(2)}, u32[]{:S(2)}) async-start(s32[2,8,8,128]{3,2,0,1:T(8,128)} %copy.42), calls=%async_computation | async-start | bytes 131072 | tf_op jit(solution)/shard_map/all_to_all | solution.py:965
  18.3 3.6 %all-to-all-done = s32[2,8,8,128]{3,2,0,1:T(8,128)S(1)} async-done(((s32[2,8,8,128]{3,2,0,1:T(8,128)}), s32[2,8,8,128]{3,2,0,1:T(8,128)S(1)}, u32[]{:S(2)}, u32[]{:S(2)}) %all-to-all-start) | async-done | bytes 65568 | tf_op jit(solution)/shard_map/all_to_all | solution.py:965
  24.2 1.9 collective-permute-start.9
  26.8 1.9 pad_maximum_fusion.4
  28.7 2.2 pad_maximum_fusion.3
  33.9 12.3 %collective-permute-done.7 = bf16[1,576,256]{2,1,0:T(8,128)(2,1)} collective-permute-done((bf16[1,576,256]{2,1,0:T(8,128)(2,1)}, bf16[1,576,256]{2,1,0:T(8,128)(2,1)}, u32[]{:S(2)}, u32[]{:S(2)}) %collective-permute-start.7) | collective-permute-done | bytes 294944 | tf_op jit(solution)/shard_map/ppermute | solution.py:938
  50.8 2.4 pad_maximum_fusion.refs_3_
  56.6 4.3 %collective-permute-start.13 = (bf16[8,576,256]{2,1,0:T(8,128)(2,1)S(1)}, bf16[8,576,256]{2,1,0:T(8,128)(2,1)}, u32[]{:S(2)}, u32[]{:S(2)}) collective-permute-start(bf16[8,576,256]{2,1,0:T(8,128)(2,1)S(1)} %constant_dynamic-update-slice_fusion.refs_4_.refs_9_), channel_id=1, source_target_pairs={{0,8},{1,9},{2,10},{3,11},{4,12},{5,13},{6,14},{7,15},{8,0},{9,1},... | collective-permute-start | bytes 7077896 | tf_op jit(solution)/shard_map/ppermute | solution.py:938
  60.8 2.4 pad_maximum_fusion.1.refs_6_.refs_11_
  63.2 2.1 collective-permute-done.16.refs_7_.refs_12_
  66.1 2.2 collective-permute-done.8
  68.3 4.2 %collective-permute-start.18 = (bf16[2,576,256]{2,1,0:T(8,128)(2,1)}, bf16[2,576,256]{2,1,0:T(8,128)(2,1)}, u32[]{:S(2)}, u32[]{:S(2)}) collective-permute-start(bf16[2,576,256]{2,1,0:T(8,128)(2,1)} %collective-permute-done.16.refs_7_.refs_12_), channel_id=1, source_target_pairs={{0,8},{1,9},{2,10},{3,11},{4,12},{5,13},{6,14},{7,15},{8,0},{9,1},... | collective-permute-start | bytes 1769480 | tf_op jit(solution)/shard_map/ppermute | solution.py:938
  74.8 2.7 %collective-permute-start.22 = (bf16[1,208,768]{2,1,0:T(8,128)(2,1)}, bf16[1,208,768]{2,1,0:T(8,128)(2,1)S(1)}, u32[]{:S(2)}, u32[]{:S(2)}) collective-permute-start(bf16[1,208,768]{2,1,0:T(8,128)(2,1)} %collective-permute-done.21.refs_5_), channel_id=1, source_target_pairs={{0,8},{1,9},{2,10},{3,11},{4,12},{5,13},{6,14},{7,15},{8,0},{9,1},... | collective-permute-start | bytes 958472 | tf_op jit(solution)/shard_map/ppermute | solution.py:938
  79.4 2.1 collective-permute-done.20.refs_7_
  82.2 7.2 %attention_forward.1 = (bf16[3,256,768]{2,1,0:T(8,128)(2,1)}, bf16[256,768]{1,0:T(8,128)(2,1)}, bf16[2,6,256,128]{3,2,1,0:T(8,128)(2,1)}, f32[256,768]{1,0:T(8,1...) custom-call(bf16[256,768]{1,0:T(8,128)(2,1)} %bitcast.35, ...), custom_call_target="tpu_custom_call" | custom-call | flops 1207959552 | bytes 14704640 | tf_op jit(solution)/shard_map/attention_forward/pallas_call | solution.py:174
  90.7 9.2 %ffn_forward.1 = (f32[256,768]{1,0:T(8,128)}, bf16[256,768]{1,0:T(8,128)(2,1)}, bf16[256,128]{1,0:T(8,128)(2,1)}, bf16[2,256,1024]{2,1,0:T(8,128)(2,1)}, bf16[2,...) custom-call(f32[256,768]{1,0:T(8,128)} %get-tuple-element.263.refs_0_.refs_1_, ...), custom_call_target="tpu_custom_call" | custom-call | flops 2415919104 | bytes 15233024 | tf_op jit(solution)/shard_map/ffn_forward/pallas_call | solution.py:174
  100.0 2.6 %collective-permute-start.25 = (bf16[256,128]{1,0:T(8,128)(2,1)}, bf16[256,128]{1,0:T(8,128)(2,1)S(1)}, u32[]{:S(2)}, u32[]{:S(2)}) collective-permute-start(bf16[256,128]{1,0:T(8,128)(2,1)} %get-tuple-element.272), channel_id=1, source_target_pairs={{0,18},{1,19},{2,16},{3,17},{4,22},{5,23},{6,20},{7,21},{8,26},{9,... | collective-permute-start | bytes 196616 | tf_op jit(solution)/shard_map/ppermute | solution.py:938
  103.9 1.6 collective-permute-start.27
  105.6 2.6 collective-permute-done.26
  108.1 1.8 collective-permute-done.27
  112.1 3.2 %collective-permute-done.28.refs_4_.refs_7_ = bf16[4,256,128]{2,1,0:T(8,128)(2,1)S(1)} collective-permute-done((bf16[4,256,128]{2,1,0:T(8,128)(2,1)S(1)}, bf16[4,256,128]{2,1,0:T(8,128)(2,1)S(1)}, u32[]{:S(2)}, u32[]{:S(2)}) %collective-permute-start.28) | collective-permute-done | bytes 262176 | tf_op jit(solution)/shard_map/ppermute | solution.py:938
  116.5 10.9 %all_to_all.10.refs_5_ = f32[8,2,8,128]{3,2,1,0:T(8,128)S(1)} all-to-all(f32[8,2,8,128]{3,2,1,0:T(8,128)S(1)} %broadcast_in_dim.89), channel_id=1, replica_groups=mesh['stream'=4,'batch'=8] {'batch'}, dimensions={0} | all-to-all | bytes 131072 | tf_op jit(solution)/shard_map/all_to_all | solution.py:1157
  128.8 9.7 %ffn_backward.1 = (f32[256,768]{1,0:T(8,128)}, f32[768,128]{1,0:T(8,128)}, f32[1,768]{1,0:T(1,128)}, bf16[2,2,256,1024]{3,2,1,0:T(8,128)(2,1)}, bf16[8,576,256]{...) custom-call(bf16[256,128]{1,0:T(8,128)(2,1)} %copy-done.8, ...), custom_call_target="tpu_custom_call" | custom-call | flops 3221225472 | bytes 27159552 | tf_op jit(solution)/shard_map/ffn_backward/pallas_call | solution.py:174
  138.6 3.9 %collective-permute-start.29 = (bf16[4,576,256]{2,1,0:T(8,128)(2,1)}, bf16[4,576,256]{2,1,0:T(8,128)(2,1)S(1)}, u32[]{:S(2)}, u32[]{:S(2)}) collective-permute-start(bf16[4,576,256]{2,1,0:T(8,128)(2,1)} %get-tuple-element.288), channel_id=1, source_target_pairs={{0,8},{1,9},{2,10},{3,11},{4,12},{5,13},{6,14},{7,15},{8,0},{9,1},... | collective-permute-start | bytes 3538952 | tf_op jit(solution)/shard_map/ppermute | solution.py:938
  142.5 2.6 %collective-permute-done.29.refs_1_ = bf16[4,576,256]{2,1,0:T(8,128)(2,1)S(1)} collective-permute-done((bf16[4,576,256]{2,1,0:T(8,128)(2,1)}, bf16[4,576,256]{2,1,0:T(8,128)(2,1)S(1)}, u32[]{:S(2)}, u32[]{:S(2)}) %collective-permute-start.29) | collective-permute-done | bytes 1179680 | tf_op jit(solution)/shard_map/ppermute | solution.py:938
  147.1 1.9 collective-permute-start.34
  148.9 8.5 %middle_backward.1 = (f32[256,768]{1,0:T(8,128)}, bf16[256,768]{1,0:T(8,128)(2,1)}, f32[1,768]{1,0:T(1,128)}) custom-call(f32[256,768]{1,0:T(8,128)} %get-tuple-element.286.refs_0_, f32[256,768]{1,0:T(8,128)} %get-tuple-element.263.refs_0_.refs_1_, bf16[2,2,256,1024]{3,2,1,0:T(8,128)(2,1)} %get-tuple-element.293.refs_2_, ...), custom_call_target="tpu_custom_call" | custom-call | flops 49999998976 | bytes 16673792 | tf_op jit(solution)/shard_map/middle_backward/pallas_call | solution.py:174
  157.5 2.5 base_up.3.refs_0_
  161.3 10.3 %attention_backward.1 = (f32[256,768]{1,0:T(8,128)}, bf16[2,208,768]{2,1,0:T(8,128)(2,1)}, bf16[6,208,768]{2,1,0:T(8,128)(2,1)}, bf16[2,208,768]{2,1,0:T(8,128)(2,1)}, bf16[6,208,768]{2,1,0:T(8,128)(2,1)}) custom-call(f32[256,768]{1,0:T(8,128)} %get-tuple-element.295.refs_0_, bf16[256,768]{1,0:T(8,128)(2,1)} %get-tuple-element.304.refs_1_, ...), custom_call_target="tpu_custom_call" | custom-call | flops 2113929216 | bytes 15398912 | tf_op jit(solution)/shard_map/attention_backward/pallas_call | solution.py:174
  172.1 2.4 base_up.5.refs_0_
  181.2 2.9 %base_up.4.refs_1_.refs_2_.refs_3_ = bf16[6,208,768]{2,1,0:T(8,128)(2,1)} custom-call(bf16[6,208,768]{2,1,0:T(8,128)(2,1)} %get-tuple-element.332.refs_0_, bf16[6,208,768]{2,1,0:T(8,128)(2,1)} %collective-permute-done.36.refs_1_), custom_call_target="tpu_custom_call" | custom-call | bytes 5750784 | tf_op jit(solution)/shard_map/base_up/pallas_call | solution.py:174
  184.1 7.8 %collective-permute-done.35.refs_2_ = bf16[2,576,256]{2,1,0:T(8,128)(2,1)} collective-permute-done((bf16[2,576,256]{2,1,0:T(8,128)(2,1)}, bf16[2,576,256]{2,1,0:T(8,128)(2,1)}, u32[]{:S(2)}, u32[]{:S(2)}) %collective-permute-start.35) | collective-permute-done | bytes 589856 | tf_op jit(solution)/shard_map/ppermute | solution.py:938
  193.2 12.3 %collective-permute-done.33.refs_0_ = bf16[2,208,768]{2,1,0:T(8,128)(2,1)} collective-permute-done((bf16[2,208,768]{2,1,0:T(8,128)(2,1)}, bf16[2,208,768]{2,1,0:T(8,128)(2,1)}, u32[]{:S(2)}, u32[]{:S(2)}) %collective-permute-start.33) | collective-permute-done | bytes 639008 | tf_op jit(solution)/shard_map/ppermute | solution.py:938
  205.6 1.7 add_up.16
  208.1 6.6 %collective-permute-done.39.refs_2_ = bf16[1,576,256]{2,1,0:T(8,128)(2,1)S(1)} collective-permute-done((bf16[1,576,256]{2,1,0:T(8,128)(2,1)S(1)}, bf16[1,576,256]{2,1,0:T(8,128)(2,1)S(1)}, u32[]{:S(2)}, u32[]{:S(2)}) %collective-permute-start.39) | collective-permute-done | bytes 294944 | tf_op jit(solution)/shard_map/ppermute | solution.py:938
  216.6 9.0 %collective-permute-done.37.refs_1_ = bf16[2,208,768]{2,1,0:T(8,128)(2,1)S(1)} collective-permute-done((bf16[2,208,768]{2,1,0:T(8,128)(2,1)S(1)}, bf16[2,208,768]{2,1,0:T(8,128)(2,1)S(1)}, u32[]{:S(2)}, u32[]{:S(2)}) %collective-permute-start.37) | collective-permute-done | bytes 639008 | tf_op jit(solution)/shard_map/ppermute | solution.py:938
  225.6 3.1 %collective-permute-done.41.refs_0_ = bf16[2,208,768]{2,1,0:T(8,128)(2,1)S(1)} collective-permute-done((bf16[2,208,768]{2,1,0:T(8,128)(2,1)S(1)}, bf16[2,208,768]{2,1,0:T(8,128)(2,1)S(1)}, u32[]{:S(2)}, u32[]{:S(2)}) %collective-permute-start.41) | collective-permute-done | bytes 639008 | tf_op jit(solution)/shard_map/ppermute | solution.py:938
  229.2 5.8 %collective-permute-done.43.refs_2_ = bf16[1,576,256]{2,1,0:T(8,128)(2,1)S(1)} collective-permute-done((bf16[1,576,256]{2,1,0:T(8,128)(2,1)S(1)}, bf16[1,576,256]{2,1,0:T(8,128)(2,1)S(1)}, u32[]{:S(2)}, u32[]{:S(2)}) %collective-permute-start.43) | collective-permute-done | bytes 294944 | tf_op jit(solution)/shard_map/ppermute | solution.py:938
  235.2 2.7 %collective-permute-start.46 = (bf16[1,576,256]{2,1,0:T(8,128)(2,1)S(1)}, bf16[1,576,256]{2,1,0:T(8,128)(2,1)S(1)}, u32[]{:S(2)}, u32[]{:S(2)}) collective-permute-start(bf16[1,576,256]{2,1,0:T(8,128)(2,1)S(1)} %add_up.20.refs_0_), channel_id=1, source_target_pairs={{0,16},{1,17},{2,18},{3,19},{4,20},{5,21},{6,22},{7,23},{8,24},{9,... | collective-permute-start | bytes 884744 | tf_op jit(solution)/shard_map/ppermute | solution.py:938
  237.9 2.9 %collective-permute-start.47 = (bf16[1,576,256]{2,1,0:T(8,128)(2,1)S(1)}, bf16[1,576,256]{2,1,0:T(8,128)(2,1)S(1)}, u32[]{:S(2)}, u32[]{:S(2)}) collective-permute-start(bf16[1,576,256]{2,1,0:T(8,128)(2,1)S(1)} %add_up.20.refs_0_), channel_id=1, source_target_pairs={{0,8},{1,9},{2,10},{3,11},{4,12},{5,13},{6,14},{7,15},{8,0},{9,1},... | collective-permute-start | bytes 884744 | tf_op jit(solution)/shard_map/ppermute | solution.py:938
  240.8 3.2 %collective-permute-done.42.refs_2_ = bf16[1,208,768]{2,1,0:T(8,128)(2,1)S(1)} collective-permute-done((bf16[1,208,768]{2,1,0:T(8,128)(2,1)S(1)}, bf16[1,208,768]{2,1,0:T(8,128)(2,1)S(1)}, u32[]{:S(2)}, u32[]{:S(2)}) %collective-permute-start.42) | collective-permute-done | bytes 319520 | tf_op jit(solution)/shard_map/ppermute | solution.py:938
  244.2 2.7 %collective-permute-start.45 = (bf16[1,208,768]{2,1,0:T(8,128)(2,1)S(1)}, bf16[1,208,768]{2,1,0:T(8,128)(2,1)S(1)}, u32[]{:S(2)}, u32[]{:S(2)}) collective-permute-start(bf16[1,208,768]{2,1,0:T(8,128)(2,1)S(1)} %add_up.21.refs_0_), channel_id=1, source_target_pairs={{0,16},{1,17},{2,18},{3,19},{4,20},{5,21},{6,22},{7,23},{8,24},{9,... | collective-permute-start | bytes 958472 | tf_op jit(solution)/shard_map/ppermute | solution.py:938
  246.9 2.7 %collective-permute-start.49 = (bf16[1,208,768]{2,1,0:T(8,128)(2,1)S(1)}, bf16[1,208,768]{2,1,0:T(8,128)(2,1)S(1)}, u32[]{:S(2)}, u32[]{:S(2)}) collective-permute-start(bf16[1,208,768]{2,1,0:T(8,128)(2,1)S(1)} %add_up.21.refs_0_), channel_id=1, source_target_pairs={{0,8},{1,9},{2,10},{3,11},{4,12},{5,13},{6,14},{7,15},{8,0},{9,1},... | collective-permute-start | bytes 958472 | tf_op jit(solution)/shard_map/ppermute | solution.py:938
  249.7 1.6 collective-permute-done.48.refs_3_
  252.4 3.0 %collective-permute-start.50 = (bf16[1,208,768]{2,1,0:T(8,128)(2,1)S(1)}, bf16[1,208,768]{2,1,0:T(8,128)(2,1)S(1)}, u32[]{:S(2)}, u32[]{:S(2)}) collective-permute-start(bf16[1,208,768]{2,1,0:T(8,128)(2,1)S(1)} %collective-permute-done.45.refs_1_), channel_id=1, source_target_pairs={{0,8},{1,9},{2,10},{3,11},{4,12},{5,13},{6,14},{7,15},{8,0},{9,1},... | collective-permute-start | bytes 958472 | tf_op jit(solution)/shard_map/ppermute | solution.py:938
  255.4 1.6 finish_wide.1
  (171 shorter events, 53.8 us)
Async XLA Ops:
  2.7 20.2 %collective-permute-start = (bf16[1,576,256]{2,1,0:T(8,128)(2,1)}, bf16[1,576,256]{2,1,0:T(8,128)(2,1)}, u32[]{:S(2)}, u32[]{:S(2)}) collective-permute-start(bf16[1,576,256]{2,1,0:T(8,128)(2,1)} %bitcast.41), channel_id=1, source_target_pairs={{0,4},{1,5},{2,6},{3,7},{4,0},{5,1},{6,2},{7,3},{8,12},{9,13},{10,... | collective-permute-start | bytes 884744 | tf_op jit(solution)/shard_map/ppermute | solution.py:938
  5.9 17.0 %collective-permute-start.1 = (bf16[1,576,256]{2,1,0:T(8,128)(2,1)}, bf16[1,576,256]{2,1,0:T(8,128)(2,1)}, u32[]{:S(2)}, u32[]{:S(2)}) collective-permute-start(bf16[1,576,256]{2,1,0:T(8,128)(2,1)} %bitcast.42), channel_id=1, source_target_pairs={{0,2},{1,3},{2,0},{3,1},{4,6},{5,7},{6,4},{7,5},{8,10},{9,11},{10,... | collective-permute-start | bytes 884744 | tf_op jit(solution)/shard_map/ppermute | solution.py:938
  7.2 15.7 %collective-permute-start.2 = (bf16[1,576,256]{2,1,0:T(8,128)(2,1)}, bf16[1,576,256]{2,1,0:T(8,128)(2,1)}, u32[]{:S(2)}, u32[]{:S(2)}) collective-permute-start(bf16[1,576,256]{2,1,0:T(8,128)(2,1)} %bitcast.43), channel_id=1, source_target_pairs={{0,16},{1,17},{2,18},{3,19},{4,20},{5,21},{6,22},{7,23},{8,24},{9,... | collective-permute-start | bytes 884744 | tf_op jit(solution)/shard_map/ppermute | solution.py:938
  8.5 14.5 %collective-permute-start.3 = (bf16[1,576,256]{2,1,0:T(8,128)(2,1)}, bf16[1,576,256]{2,1,0:T(8,128)(2,1)}, u32[]{:S(2)}, u32[]{:S(2)}) collective-permute-start(bf16[1,576,256]{2,1,0:T(8,128)(2,1)} %bitcast.44), channel_id=1, source_target_pairs={{0,1},{1,0},{2,3},{3,2},{4,5},{5,4},{6,7},{7,6},{8,9},{9,8},{10,11... | collective-permute-start | bytes 884744 | tf_op jit(solution)/shard_map/ppermute | solution.py:938
  10.3 11.6 %all-to-all-start = ((s32[2,8,8,128]{3,2,0,1:T(8,128)}), s32[2,8,8,128]{3,2,0,1:T(8,128)S(1)}, u32[]{:S(2)}, u32[]{:S(2)}) async-start(s32[2,8,8,128]{3,2,0,1:T(8,128)} %copy.42), calls=%async_computation | async-start | bytes 131072 | tf_op jit(solution)/shard_map/all_to_all | solution.py:965
  13.7 10.5 %collective-permute-start.4 = (bf16[1,208,768]{2,1,0:T(8,128)(2,1)}, bf16[1,208,768]{2,1,0:T(8,128)(2,1)}, u32[]{:S(2)}, u32[]{:S(2)}) collective-permute-start(bf16[1,208,768]{2,1,0:T(8,128)(2,1)} %bitcast.37), channel_id=1, source_target_pairs={{0,1},{1,0},{2,3},{3,2},{4,5},{5,4},{6,7},{7,6},{8,9},{9,8},{10,11... | collective-permute-start | bytes 958472 | tf_op jit(solution)/shard_map/ppermute | solution.py:938
  24.2 25.0 %collective-permute-start.5 = (bf16[1,208,768]{2,1,0:T(8,128)(2,1)}, bf16[1,208,768]{2,1,0:T(8,128)(2,1)}, u32[]{:S(2)}, u32[]{:S(2)}) collective-permute-start(bf16[1,208,768]{2,1,0:T(8,128)(2,1)} %bitcast.38), channel_id=1, source_target_pairs={{0,2},{1,3},{2,0},{3,1},{4,6},{5,7},{6,4},{7,5},{8,10},{9,11},{10,... | collective-permute-start | bytes 958472 | tf_op jit(solution)/shard_map/ppermute | solution.py:938
  24.2 25.0 %collective-permute-start.9 = (bf16[1,208,768]{2,1,0:T(8,128)(2,1)}, bf16[1,208,768]{2,1,0:T(8,128)(2,1)}, u32[]{:S(2)}, u32[]{:S(2)}) collective-permute-start(bf16[1,208,768]{2,1,0:T(8,128)(2,1)} %bitcast.39), channel_id=1, source_target_pairs={{0,4},{1,5},{2,6},{3,7},{4,0},{5,1},{6,2},{7,3},{8,12},{9,13},{10,... | collective-permute-start | bytes 958472 | tf_op jit(solution)/shard_map/ppermute | solution.py:938
  26.1 20.0 %collective-permute-start.7 = (bf16[1,576,256]{2,1,0:T(8,128)(2,1)}, bf16[1,576,256]{2,1,0:T(8,128)(2,1)}, u32[]{:S(2)}, u32[]{:S(2)}) collective-permute-start(bf16[1,576,256]{2,1,0:T(8,128)(2,1)} %collective-permute-done), channel_id=1, source_target_pairs={{0,2},{1,3},{2,0},{3,1},{4,6},{5,7},{6,4},{7,5},{8,10},{9,11},{10,... | collective-permute-start | bytes 884744 | tf_op jit(solution)/shard_map/ppermute | solution.py:938
  30.8 15.3 %collective-permute-start.6 = (bf16[2,576,256]{2,1,0:T(8,128)(2,1)}, bf16[2,576,256]{2,1,0:T(8,128)(2,1)}, u32[]{:S(2)}, u32[]{:S(2)}) collective-permute-start(bf16[2,576,256]{2,1,0:T(8,128)(2,1)} %pad_maximum_fusion.4), channel_id=1, source_target_pairs={{0,1},{1,0},{2,3},{3,2},{4,5},{5,4},{6,7},{7,6},{8,9},{9,8},{10,11... | collective-permute-start | bytes 1769480 | tf_op jit(solution)/shard_map/ppermute | solution.py:938
  31.4 21.8 %collective-permute-start.12 = (bf16[3,576,256]{2,1,0:T(8,128)(2,1)}, bf16[3,576,256]{2,1,0:T(8,128)(2,1)}, u32[]{:S(2)}, u32[]{:S(2)}) collective-permute-start(bf16[3,576,256]{2,1,0:T(8,128)(2,1)} %pad_maximum_fusion.3), channel_id=1, source_target_pairs={{0,16},{1,17},{2,18},{3,19},{4,20},{5,21},{6,22},{7,23},{8,24},{9,... | collective-permute-start | bytes 2654216 | tf_op jit(solution)/shard_map/ppermute | solution.py:938
  47.2 7.4 %collective-permute-start.11 = (bf16[1,576,256]{2,1,0:T(8,128)(2,1)}, bf16[1,576,256]{2,1,0:T(8,128)(2,1)S(1)}, u32[]{:S(2)}, u32[]{:S(2)}) collective-permute-start(bf16[1,576,256]{2,1,0:T(8,128)(2,1)} %collective-permute-done.7), channel_id=1, source_target_pairs={{0,1},{1,0},{2,3},{3,2},{4,5},{5,4},{6,7},{7,6},{8,9},{9,8},{10,11... | collective-permute-start | bytes 884744 | tf_op jit(solution)/shard_map/ppermute | solution.py:938
  49.2 14.0 %collective-permute-start.14 = (bf16[1,208,768]{2,1,0:T(8,128)(2,1)}, bf16[1,208,768]{2,1,0:T(8,128)(2,1)}, u32[]{:S(2)}, u32[]{:S(2)}) collective-permute-start(bf16[1,208,768]{2,1,0:T(8,128)(2,1)} %collective-permute-done.9), channel_id=1, source_target_pairs={{0,2},{1,3},{2,0},{3,1},{4,6},{5,7},{6,4},{7,5},{8,10},{9,11},{10,... | collective-permute-start | bytes 958472 | tf_op jit(solution)/shard_map/ppermute | solution.py:938
  49.3 16.8 %collective-permute-start.10 = (bf16[1,208,768]{2,1,0:T(8,128)(2,1)}, bf16[1,208,768]{2,1,0:T(8,128)(2,1)}, u32[]{:S(2)}, u32[]{:S(2)}) collective-permute-start(bf16[1,208,768]{2,1,0:T(8,128)(2,1)} %collective-permute-done.9), channel_id=1, source_target_pairs={{0,1},{1,0},{2,3},{3,2},{4,5},{5,4},{6,7},{7,6},{8,9},{9,8},{10,11... | collective-permute-start | bytes 958472 | tf_op jit(solution)/shard_map/ppermute | solution.py:938
  49.9 18.4 %collective-permute-start.8 = (bf16[1,208,768]{2,1,0:T(8,128)(2,1)}, bf16[1,208,768]{2,1,0:T(8,128)(2,1)}, u32[]{:S(2)}, u32[]{:S(2)}) collective-permute-start(bf16[1,208,768]{2,1,0:T(8,128)(2,1)} %collective-permute-done.5), channel_id=1, source_target_pairs={{0,1},{1,0},{2,3},{3,2},{4,5},{5,4},{6,7},{7,6},{8,9},{9,8},{10,11... | collective-permute-start | bytes 958472 | tf_op jit(solution)/shard_map/ppermute | solution.py:938
  53.2 12.1 %collective-permute-start.16 = (bf16[2,576,256]{2,1,0:T(8,128)(2,1)S(1)}, bf16[2,576,256]{2,1,0:T(8,128)(2,1)}, u32[]{:S(2)}, u32[]{:S(2)}) collective-permute-start(bf16[2,576,256]{2,1,0:T(8,128)(2,1)S(1)} %pad_maximum_fusion.5), channel_id=1, source_target_pairs={{0,16},{1,17},{2,18},{3,19},{4,20},{5,21},{6,22},{7,23},{8,24},{9,... | collective-permute-start | bytes 1769480 | tf_op jit(solution)/shard_map/ppermute | solution.py:938
  56.6 15.9 %collective-permute-start.13 = (bf16[8,576,256]{2,1,0:T(8,128)(2,1)S(1)}, bf16[8,576,256]{2,1,0:T(8,128)(2,1)}, u32[]{:S(2)}, u32[]{:S(2)}) collective-permute-start(bf16[8,576,256]{2,1,0:T(8,128)(2,1)S(1)} %constant_dynamic-update-slice_fusion.refs_4_.refs_9_), channel_id=1, source_target_pairs={{0,8},{1,9},{2,10},{3,11},{4,12},{5,13},{6,14},{7,15},{8,0},{9,1},... | collective-permute-start | bytes 7077896 | tf_op jit(solution)/shard_map/ppermute | solution.py:938
  63.2 9.3 %collective-permute-start.15 = (bf16[4,208,768]{2,1,0:T(8,128)(2,1)}, bf16[4,208,768]{2,1,0:T(8,128)(2,1)}, u32[]{:S(2)}, u32[]{:S(2)}) collective-permute-start(bf16[4,208,768]{2,1,0:T(8,128)(2,1)} %pad_maximum_fusion.refs_3_), channel_id=1, source_target_pairs={{0,8},{1,9},{2,10},{3,11},{4,12},{5,13},{6,14},{7,15},{8,0},{9,1},... | collective-permute-start | bytes 3833864 | tf_op jit(solution)/shard_map/ppermute | solution.py:938
  65.4 9.4 %collective-permute-start.21 = (bf16[1,208,768]{2,1,0:T(8,128)(2,1)}, bf16[1,208,768]{2,1,0:T(8,128)(2,1)}, u32[]{:S(2)}, u32[]{:S(2)}) collective-permute-start(bf16[1,208,768]{2,1,0:T(8,128)(2,1)} %collective-permute-done.14), channel_id=1, source_target_pairs={{0,1},{1,0},{2,3},{3,2},{4,5},{5,4},{6,7},{7,6},{8,9},{9,8},{10,11... | collective-permute-start | bytes 958472 | tf_op jit(solution)/shard_map/ppermute | solution.py:938
  66.1 11.9 %collective-permute-start.19 = (bf16[2,576,256]{2,1,0:T(8,128)(2,1)}, bf16[2,576,256]{2,1,0:T(8,128)(2,1)}, u32[]{:S(2)}, u32[]{:S(2)}) collective-permute-start(bf16[2,576,256]{2,1,0:T(8,128)(2,1)} %pad_maximum_fusion.6), channel_id=1, source_target_pairs={{0,16},{1,17},{2,18},{3,19},{4,20},{5,21},{6,22},{7,23},{8,24},{9,... | collective-permute-start | bytes 1769480 | tf_op jit(solution)/shard_map/ppermute | solution.py:938
  68.3 21.2 %collective-permute-start.18 = (bf16[2,576,256]{2,1,0:T(8,128)(2,1)}, bf16[2,576,256]{2,1,0:T(8,128)(2,1)}, u32[]{:S(2)}, u32[]{:S(2)}) collective-permute-start(bf16[2,576,256]{2,1,0:T(8,128)(2,1)} %collective-permute-done.16.refs_7_.refs_12_), channel_id=1, source_target_pairs={{0,8},{1,9},{2,10},{3,11},{4,12},{5,13},{6,14},{7,15},{8,0},{9,1},... | collective-permute-start | bytes 1769480 | tf_op jit(solution)/shard_map/ppermute | solution.py:938
  74.8 4.6 %collective-permute-start.22 = (bf16[1,208,768]{2,1,0:T(8,128)(2,1)}, bf16[1,208,768]{2,1,0:T(8,128)(2,1)S(1)}, u32[]{:S(2)}, u32[]{:S(2)}) collective-permute-start(bf16[1,208,768]{2,1,0:T(8,128)(2,1)} %collective-permute-done.21.refs_5_), channel_id=1, source_target_pairs={{0,8},{1,9},{2,10},{3,11},{4,12},{5,13},{6,14},{7,15},{8,0},{9,1},... | collective-permute-start | bytes 958472 | tf_op jit(solution)/shard_map/ppermute | solution.py:938
  77.5 11.9 %collective-permute-start.17 = (bf16[4,576,256]{2,1,0:T(8,128)(2,1)}, bf16[4,576,256]{2,1,0:T(8,128)(2,1)S(1)}, u32[]{:S(2)}, u32[]{:S(2)}) collective-permute-start(bf16[4,576,256]{2,1,0:T(8,128)(2,1)} %pad_maximum_fusion.1.refs_6_.refs_11_), channel_id=1, source_target_pairs={{0,8},{1,9},{2,10},{3,11},{4,12},{5,13},{6,14},{7,15},{8,0},{9,1},... | collective-permute-start | bytes 3538952 | tf_op jit(solution)/shard_map/ppermute | solution.py:938
  81.5 8.0 %collective-permute-start.23 = (bf16[2,576,256]{2,1,0:T(8,128)(2,1)}, bf16[2,576,256]{2,1,0:T(8,128)(2,1)S(1)}, u32[]{:S(2)}, u32[]{:S(2)}) collective-permute-start(bf16[2,576,256]{2,1,0:T(8,128)(2,1)} %collective-permute-done.19.refs_8_.refs_13_), channel_id=1, source_target_pairs={{0,8},{1,9},{2,10},{3,11},{4,12},{5,13},{6,14},{7,15},{8,0},{9,1},... | collective-permute-start | bytes 1769480 | tf_op jit(solution)/shard_map/ppermute | solution.py:938
  99.9 5.7 %collective-permute-start.24 = (bf16[256,128]{1,0:T(8,128)(2,1)}, bf16[256,128]{1,0:T(8,128)(2,1)S(1)}, u32[]{:S(2)}, u32[]{:S(2)}) collective-permute-start(bf16[256,128]{1,0:T(8,128)(2,1)} %get-tuple-element.272), channel_id=1, source_target_pairs={{0,16},{1,17},{2,18},{3,19},{4,20},{5,21},{6,22},{7,23},{8,24},{9,... | collective-permute-start | bytes 196616 | tf_op jit(solution)/shard_map/ppermute | solution.py:938
  100.0 5.6 %collective-permute-start.25 = (bf16[256,128]{1,0:T(8,128)(2,1)}, bf16[256,128]{1,0:T(8,128)(2,1)S(1)}, u32[]{:S(2)}, u32[]{:S(2)}) collective-permute-start(bf16[256,128]{1,0:T(8,128)(2,1)} %get-tuple-element.272), channel_id=1, source_target_pairs={{0,18},{1,19},{2,16},{3,17},{4,22},{5,23},{6,20},{7,21},{8,26},{9,... | collective-permute-start | bytes 196616 | tf_op jit(solution)/shard_map/ppermute | solution.py:938
  102.6 5.6 %collective-permute-start.26 = (bf16[256,128]{1,0:T(8,128)(2,1)}, bf16[256,128]{1,0:T(8,128)(2,1)S(1)}, u32[]{:S(2)}, u32[]{:S(2)}) collective-permute-start(bf16[256,128]{1,0:T(8,128)(2,1)} %get-tuple-element.272), channel_id=1, source_target_pairs={{0,20},{1,21},{2,22},{3,23},{4,16},{5,17},{6,18},{7,19},{8,28},{9,... | collective-permute-start | bytes 196616 | tf_op jit(solution)/shard_map/ppermute | solution.py:938
  103.9 6.0 %collective-permute-start.27 = (bf16[256,128]{1,0:T(8,128)(2,1)}, bf16[256,128]{1,0:T(8,128)(2,1)S(1)}, u32[]{:S(2)}, u32[]{:S(2)}) collective-permute-start(bf16[256,128]{1,0:T(8,128)(2,1)} %get-tuple-element.272), channel_id=1, source_target_pairs={{0,22},{1,23},{2,20},{3,21},{4,18},{5,19},{6,16},{7,17},{8,30},{9,... | collective-permute-start | bytes 196616 | tf_op jit(solution)/shard_map/ppermute | solution.py:938
  110.0 5.3 %collective-permute-start.28 = (bf16[4,256,128]{2,1,0:T(8,128)(2,1)S(1)}, bf16[4,256,128]{2,1,0:T(8,128)(2,1)S(1)}, u32[]{:S(2)}, u32[]{:S(2)}) collective-permute-start(bf16[4,256,128]{2,1,0:T(8,128)(2,1)S(1)} %pad_maximum_fusion.7.refs_3_.refs_6_), channel_id=1, source_target_pairs={{0,1},{1,0},{2,3},{3,2},{4,5},{5,4},{6,7},{7,6},{8,9},{9,8},{10,11... | collective-permute-start | bytes 786440 | tf_op jit(solution)/shard_map/ppermute | solution.py:938
  138.6 6.6 %collective-permute-start.29 = (bf16[4,576,256]{2,1,0:T(8,128)(2,1)}, bf16[4,576,256]{2,1,0:T(8,128)(2,1)S(1)}, u32[]{:S(2)}, u32[]{:S(2)}) collective-permute-start(bf16[4,576,256]{2,1,0:T(8,128)(2,1)} %get-tuple-element.288), channel_id=1, source_target_pairs={{0,8},{1,9},{2,10},{3,11},{4,12},{5,13},{6,14},{7,15},{8,0},{9,1},... | collective-permute-start | bytes 3538952 | tf_op jit(solution)/shard_map/ppermute | solution.py:938
  142.5 15.0 %collective-permute-start.30 = (bf16[4,576,256]{2,1,0:T(8,128)(2,1)}, bf16[4,576,256]{2,1,0:T(8,128)(2,1)S(1)}, u32[]{:S(2)}, u32[]{:S(2)}) collective-permute-start(bf16[4,576,256]{2,1,0:T(8,128)(2,1)} %get-tuple-element.297), channel_id=1, source_target_pairs={{0,8},{1,9},{2,10},{3,11},{4,12},{5,13},{6,14},{7,15},{8,0},{9,1},... | collective-permute-start | bytes 3538952 | tf_op jit(solution)/shard_map/ppermute | solution.py:938
  145.1 12.3 %collective-permute-start.31 = (bf16[8,576,256]{2,1,0:T(8,128)(2,1)}, bf16[8,576,256]{2,1,0:T(8,128)(2,1)}, u32[]{:S(2)}, u32[]{:S(2)}) collective-permute-start(bf16[8,576,256]{2,1,0:T(8,128)(2,1)} %get-tuple-element.298), channel_id=1, source_target_pairs={{0,8},{1,9},{2,10},{3,11},{4,12},{5,13},{6,14},{7,15},{8,0},{9,1},... | collective-permute-start | bytes 7077896 | tf_op jit(solution)/shard_map/ppermute | solution.py:938
  147.1 28.4 %collective-permute-start.34 = (bf16[4,576,256]{2,1,0:T(8,128)(2,1)S(1)}, bf16[4,576,256]{2,1,0:T(8,128)(2,1)S(1)}, u32[]{:S(2)}, u32[]{:S(2)}) collective-permute-start(bf16[4,576,256]{2,1,0:T(8,128)(2,1)S(1)} %add_up.11), channel_id=1, source_target_pairs={{0,16},{1,17},{2,18},{3,19},{4,20},{5,21},{6,22},{7,23},{8,24},{9,... | collective-permute-start | bytes 3538952 | tf_op jit(solution)/shard_map/ppermute | solution.py:938
  177.1 14.8 %collective-permute-start.35 = (bf16[2,576,256]{2,1,0:T(8,128)(2,1)}, bf16[2,576,256]{2,1,0:T(8,128)(2,1)}, u32[]{:S(2)}, u32[]{:S(2)}) collective-permute-start(bf16[2,576,256]{2,1,0:T(8,128)(2,1)} %add_up.14), channel_id=1, source_target_pairs={{0,1},{1,0},{2,3},{3,2},{4,5},{5,4},{6,7},{7,6},{8,9},{9,8},{10,11... | collective-permute-start | bytes 1769480 | tf_op jit(solution)/shard_map/ppermute | solution.py:938
  177.2 28.4 %collective-permute-start.33 = (bf16[2,208,768]{2,1,0:T(8,128)(2,1)}, bf16[2,208,768]{2,1,0:T(8,128)(2,1)}, u32[]{:S(2)}, u32[]{:S(2)}) collective-permute-start(bf16[2,208,768]{2,1,0:T(8,128)(2,1)} %add_up.13), channel_id=1, source_target_pairs={{0,1},{1,0},{2,3},{3,2},{4,5},{5,4},{6,7},{7,6},{8,9},{9,8},{10,11... | collective-permute-start | bytes 1916936 | tf_op jit(solution)/shard_map/ppermute | solution.py:938
  178.5 28.7 %collective-permute-start.38 = (bf16[4,576,256]{2,1,0:T(8,128)(2,1)}, bf16[4,576,256]{2,1,0:T(8,128)(2,1)S(1)}, u32[]{:S(2)}, u32[]{:S(2)}) collective-permute-start(bf16[4,576,256]{2,1,0:T(8,128)(2,1)} %add_up.12), channel_id=1, source_target_pairs={{0,16},{1,17},{2,18},{3,19},{4,20},{5,21},{6,22},{7,23},{8,24},{9,... | collective-permute-start | bytes 3538952 | tf_op jit(solution)/shard_map/ppermute | solution.py:938
  193.2 21.6 %collective-permute-start.40 = (bf16[2,576,256]{2,1,0:T(8,128)(2,1)S(1)}, bf16[2,576,256]{2,1,0:T(8,128)(2,1)S(1)}, u32[]{:S(2)}, u32[]{:S(2)}) collective-permute-start(bf16[2,576,256]{2,1,0:T(8,128)(2,1)S(1)} %add_up.15), channel_id=1, source_target_pairs={{0,2},{1,3},{2,0},{3,1},{4,6},{5,7},{6,4},{7,5},{8,10},{9,11},{10,... | collective-permute-start | bytes 1769480 | tf_op jit(solution)/shard_map/ppermute | solution.py:938
  207.4 7.3 %collective-permute-start.39 = (bf16[1,576,256]{2,1,0:T(8,128)(2,1)S(1)}, bf16[1,576,256]{2,1,0:T(8,128)(2,1)S(1)}, u32[]{:S(2)}, u32[]{:S(2)}) collective-permute-start(bf16[1,576,256]{2,1,0:T(8,128)(2,1)S(1)} %get-tuple-element.351), channel_id=1, source_target_pairs={{0,1},{1,0},{2,3},{3,2},{4,5},{5,4},{6,7},{7,6},{8,9},{9,8},{10,11... | collective-permute-start | bytes 884744 | tf_op jit(solution)/shard_map/ppermute | solution.py:938
  207.6 18.0 %collective-permute-start.37 = (bf16[2,208,768]{2,1,0:T(8,128)(2,1)S(1)}, bf16[2,208,768]{2,1,0:T(8,128)(2,1)S(1)}, u32[]{:S(2)}, u32[]{:S(2)}) collective-permute-start(bf16[2,208,768]{2,1,0:T(8,128)(2,1)S(1)} %get-tuple-element.344), channel_id=1, source_target_pairs={{0,2},{1,3},{2,0},{3,1},{4,6},{5,7},{6,4},{7,5},{8,10},{9,11},{10,... | collective-permute-start | bytes 1916936 | tf_op jit(solution)/shard_map/ppermute | solution.py:938
  214.9 13.8 %collective-permute-start.41 = (bf16[2,208,768]{2,1,0:T(8,128)(2,1)S(1)}, bf16[2,208,768]{2,1,0:T(8,128)(2,1)S(1)}, u32[]{:S(2)}, u32[]{:S(2)}) collective-permute-start(bf16[2,208,768]{2,1,0:T(8,128)(2,1)S(1)} %get-tuple-element.359), channel_id=1, source_target_pairs={{0,1},{1,0},{2,3},{3,2},{4,5},{5,4},{6,7},{7,6},{8,9},{9,8},{10,11... | collective-permute-start | bytes 1916936 | tf_op jit(solution)/shard_map/ppermute | solution.py:938
  215.1 19.9 %collective-permute-start.43 = (bf16[1,576,256]{2,1,0:T(8,128)(2,1)S(1)}, bf16[1,576,256]{2,1,0:T(8,128)(2,1)S(1)}, u32[]{:S(2)}, u32[]{:S(2)}) collective-permute-start(bf16[1,576,256]{2,1,0:T(8,128)(2,1)S(1)} %get-tuple-element.365), channel_id=1, source_target_pairs={{0,1},{1,0},{2,3},{3,2},{4,5},{5,4},{6,7},{7,6},{8,9},{9,8},{10,11... | collective-permute-start | bytes 884744 | tf_op jit(solution)/shard_map/ppermute | solution.py:938
  216.5 18.6 %collective-permute-start.44 = (bf16[1,576,256]{2,1,0:T(8,128)(2,1)S(1)}, bf16[1,576,256]{2,1,0:T(8,128)(2,1)S(1)}, u32[]{:S(2)}, u32[]{:S(2)}) collective-permute-start(bf16[1,576,256]{2,1,0:T(8,128)(2,1)S(1)} %add_up.18), channel_id=1, source_target_pairs={{0,4},{1,5},{2,6},{3,7},{4,0},{5,1},{6,2},{7,3},{8,12},{9,13},{10,... | collective-permute-start | bytes 884744 | tf_op jit(solution)/shard_map/ppermute | solution.py:938
  228.9 15.0 %collective-permute-start.42 = (bf16[1,208,768]{2,1,0:T(8,128)(2,1)S(1)}, bf16[1,208,768]{2,1,0:T(8,128)(2,1)S(1)}, u32[]{:S(2)}, u32[]{:S(2)}) collective-permute-start(bf16[1,208,768]{2,1,0:T(8,128)(2,1)S(1)} %add_up.19), channel_id=1, source_target_pairs={{0,4},{1,5},{2,6},{3,7},{4,0},{5,1},{6,2},{7,3},{8,12},{9,13},{10,... | collective-permute-start | bytes 958472 | tf_op jit(solution)/shard_map/ppermute | solution.py:938
  235.2 14.3 %collective-permute-start.46 = (bf16[1,576,256]{2,1,0:T(8,128)(2,1)S(1)}, bf16[1,576,256]{2,1,0:T(8,128)(2,1)S(1)}, u32[]{:S(2)}, u32[]{:S(2)}) collective-permute-start(bf16[1,576,256]{2,1,0:T(8,128)(2,1)S(1)} %add_up.20.refs_0_), channel_id=1, source_target_pairs={{0,16},{1,17},{2,18},{3,19},{4,20},{5,21},{6,22},{7,23},{8,24},{9,... | collective-permute-start | bytes 884744 | tf_op jit(solution)/shard_map/ppermute | solution.py:938
  237.9 11.7 %collective-permute-start.47 = (bf16[1,576,256]{2,1,0:T(8,128)(2,1)S(1)}, bf16[1,576,256]{2,1,0:T(8,128)(2,1)S(1)}, u32[]{:S(2)}, u32[]{:S(2)}) collective-permute-start(bf16[1,576,256]{2,1,0:T(8,128)(2,1)S(1)} %add_up.20.refs_0_), channel_id=1, source_target_pairs={{0,8},{1,9},{2,10},{3,11},{4,12},{5,13},{6,14},{7,15},{8,0},{9,1},... | collective-permute-start | bytes 884744 | tf_op jit(solution)/shard_map/ppermute | solution.py:938
  244.2 8.2 %collective-permute-start.45 = (bf16[1,208,768]{2,1,0:T(8,128)(2,1)S(1)}, bf16[1,208,768]{2,1,0:T(8,128)(2,1)S(1)}, u32[]{:S(2)}, u32[]{:S(2)}) collective-permute-start(bf16[1,208,768]{2,1,0:T(8,128)(2,1)S(1)} %add_up.21.refs_0_), channel_id=1, source_target_pairs={{0,16},{1,17},{2,18},{3,19},{4,20},{5,21},{6,22},{7,23},{8,24},{9,... | collective-permute-start | bytes 958472 | tf_op jit(solution)/shard_map/ppermute | solution.py:938
  246.9 5.5 %collective-permute-start.49 = (bf16[1,208,768]{2,1,0:T(8,128)(2,1)S(1)}, bf16[1,208,768]{2,1,0:T(8,128)(2,1)S(1)}, u32[]{:S(2)}, u32[]{:S(2)}) collective-permute-start(bf16[1,208,768]{2,1,0:T(8,128)(2,1)S(1)} %add_up.21.refs_0_), channel_id=1, source_target_pairs={{0,8},{1,9},{2,10},{3,11},{4,12},{5,13},{6,14},{7,15},{8,0},{9,1},... | collective-permute-start | bytes 958472 | tf_op jit(solution)/shard_map/ppermute | solution.py:938
  252.4 4.6 %collective-permute-start.50 = (bf16[1,208,768]{2,1,0:T(8,128)(2,1)S(1)}, bf16[1,208,768]{2,1,0:T(8,128)(2,1)S(1)}, u32[]{:S(2)}, u32[]{:S(2)}) collective-permute-start(bf16[1,208,768]{2,1,0:T(8,128)(2,1)S(1)} %collective-permute-done.45.refs_1_), channel_id=1, source_target_pairs={{0,8},{1,9},{2,10},{3,11},{4,12},{5,13},{6,14},{7,15},{8,0},{9,1},... | collective-permute-start | bytes 958472 | tf_op jit(solution)/shard_map/ppermute | solution.py:938
  (23 other events, 181.2 us)
